TPU v7x, 128 devices: a whole 4x4x4 slice. The times are simulated.
128 devices in a mesh: row: 8 (over x, core), col: 16 (over y, z).
Axes of the slice: x: 4, y: 4, z: 4, core: 2. Of those that a mesh axis runs over, the one named last changes fastest.
Arguments:
- node_feats: bfloat16 [65536, 256], P(('row', 'col')), may hold values from -6 to 6
- out_grad: bfloat16 [65536, 256], P(('row', 'col')), may hold values from -6 to 6
- weight_one: bfloat16 [256, 256], replicated, may hold values from -0.375 to 0.375
- weight_two: bfloat16 [256, 256], replicated, may hold values from -0.375 to 0.375
- tile_values: bfloat16 [16384, 256, 256], P(('row', 'col')), may hold values from -0.09375 to 0.09375
- tile_rows: int32 [16384], P(('row', 'col')), may hold values from 0 to 31, as said below
- tile_cols: int32 [16384], P(('row', 'col')), may hold values from 0 to 15
- tile_count: int32 [128], P(('row', 'col')), may hold values from 1 to 128, as said below
Outputs:
- input_grad: bfloat16 [65536, 256], P(('row', 'col'))
- grad_one: float32 [256, 256], replicated
- grad_two: float32 [256, 256], replicated
Inputs may be any that keep to these rules, and one draw needn't show every extreme that they name: Within one device's slots the pairs (tile_rows, tile_cols) are all different. `tile_count`: some device has all 128 slots live.
All inputs are finite; a program needn't handle non-finite values.
Results may differ from a plain program's by a relative error of at most 0.0085.
Values may be sent and summed in bfloat16 or wider, within the bound.
A program may use at most 192 MiB of HBM per device.

v0:
```python
import jax
import jax.numpy as jnp
from jax import lax
from jax.sharding import PartitionSpec as P


def forward_product(tile_values, tile_rows, tile_cols, live, shard):
    tile_size = tile_values.shape[1]
    feat_width = shard.shape[1]
    gathered = lax.all_gather(shard, "row", axis=0, tiled=True)
    blocks = gathered.reshape(-1, tile_size, feat_width)
    picked = blocks[tile_cols]
    product = jnp.einsum("tij,tjf->tif", tile_values, picked, preferred_element_type=jnp.float32)
    product = product * live.astype(jnp.float32)[:, None, None]
    row_blocks = lax.axis_size("col") * (shard.shape[0] // tile_size)
    selector = (tile_rows[None, :] == jnp.arange(row_blocks)[:, None]).astype(jnp.float32)
    partial_value = jnp.einsum("rt,tif->rif", selector, product, precision=lax.Precision.HIGHEST)
    return lax.psum_scatter(
        partial_value.reshape(-1, feat_width), "col", scatter_dimension=0, tiled=True
    )


def transposed_product(tile_values, tile_rows, tile_cols, live, shard):
    tile_size = tile_values.shape[1]
    feat_width = shard.shape[1]
    gathered = lax.all_gather(shard, "col", axis=0, tiled=True)
    blocks = gathered.reshape(-1, tile_size, feat_width)
    picked = blocks[tile_rows]
    product = jnp.einsum("tji,tjf->tif", tile_values, picked, preferred_element_type=jnp.float32)
    col_blocks = lax.axis_size("row") * (shard.shape[0] // tile_size)
    selector = ((tile_cols[None, :] == jnp.arange(col_blocks)[:, None]) & live[None, :]).astype(
        jnp.float32
    )
    partial_value = jnp.einsum("rt,tif->rif", selector, product, precision=lax.Precision.HIGHEST)
    return lax.psum_scatter(
        partial_value.reshape(-1, feat_width), "row", scatter_dimension=0, tiled=True
    )


def per_device(
    node_feats, out_grad, weight_one, weight_two, tile_values, tile_rows, tile_cols, tile_count
):
    slot_total = tile_values.shape[0]
    live = jnp.arange(slot_total, dtype=jnp.int32) < tile_count[0]
    projected = jnp.dot(node_feats, weight_one, preferred_element_type=jnp.float32).astype(
        jnp.bfloat16
    )
    pre_act = forward_product(tile_values, tile_rows, tile_cols, live, projected)
    back_two = transposed_product(tile_values, tile_rows, tile_cols, live, out_grad).astype(
        jnp.bfloat16
    )
    hidden = jax.nn.silu(pre_act).astype(jnp.bfloat16)
    grad_two = jnp.einsum("nf,ng->fg", hidden, back_two, preferred_element_type=jnp.float32)
    grad_two = lax.psum(grad_two, ("row", "col"))
    d_hidden = jnp.dot(back_two, weight_two.T, preferred_element_type=jnp.float32)
    sigma = jax.nn.sigmoid(pre_act)
    grad_pre = (d_hidden * sigma * (1.0 + pre_act * (1.0 - sigma))).astype(jnp.bfloat16)
    back_one = transposed_product(tile_values, tile_rows, tile_cols, live, grad_pre).astype(
        jnp.bfloat16
    )
    grad_one = jnp.einsum("nf,ng->fg", node_feats, back_one, preferred_element_type=jnp.float32)
    input_grad = jnp.dot(back_one, weight_one.T, preferred_element_type=jnp.float32).astype(
        jnp.bfloat16
    )
    grad_one = lax.psum(grad_one, ("row", "col"))
    return (input_grad, grad_one, grad_two)


def solution(mesh):
    in_specs = (
        P(("row", "col"), None),
        P(("row", "col"), None),
        P(),
        P(),
        P(("row", "col"), None, None),
        P(("row", "col")),
        P(("row", "col")),
        P(("row", "col")),
    )
    out_specs = (P(("row", "col"), None), P(), P())
    return jax.shard_map(
        per_device, mesh=mesh, in_specs=in_specs, out_specs=out_specs, check_vma=False
    )
```

profile of v0, /device:TPU:0, one launch (start us, length us, event | category | flops | bytes accessed | tf_op | source)
XLA Modules:
  0.0 685.4 jit_solution(12516936670211974651)
XLA Ops:
  8.1 1.8 convolution_convert_fusion.1
  11.4 53.0 %all-gather.4.cloned.1.call-done = bf16[8192,256]{1,0:T(8,128)(2,1)} async-done(((bf16[512,256]{1,0:T(8,128)(2,1)}), bf16[8192,256]{1,0:T(8,128)(2,1)}) %all-gather.4.cloned.1.call-update) | async-done | bytes 4194320 | tf_op jit(solution)/shard_map/all_gather | solution.py:26
  64.3 10.6 %gather_fusion = bf16[128,256,256]{2,1,0:T(8,128)(2,1)} fusion(bf16[32,256,256]{2,1,0:T(8,128)(2,1)} %bitcast.38, s32[1024]{0:T(1024)S(1)} %pad_clamp_fusion.1), kind=kCustom, calls=%fused_computation | custom fusion | bytes 33554944 | tf_op jit(solution)/shard_map/gather | solution.py:28
  74.9 24.8 %fusion.28 = f32[128,256,256]{2,1,0:T(8,128)} fusion(bf16[128,256,256]{2,1,0:T(8,128)(2,1)} %gather_fusion, bf16[128,256,256]{2,1,0:T(8,128)(2,1)} %param.12), kind=kOutput, calls=%fused_computation.41 | convolution fusion | flops 4294967296 | bytes 67108864 | tf_op jit(solution)/shard_map/tji,tjf->tif/dot_general | solution.py:29
  99.7 34.1 %copy.17 = f32[128,256,256]{1,0,2:T(8,128)} copy(f32[128,256,256]{2,1,0:T(8,128)} %fusion.28) | data formatting | bytes 67108864 | tf_op jit(solution)/shard_map/tji,tjf->tif/dot_general | solution.py:29
  133.9 17.5 %fusion.4 = f32[16,256,256]{2,0,1:T(8,128)} fusion(f32[128,256,256]{1,0,2:T(8,128)} %copy.17, s32[128]{0:T(128)S(1)} %copy-done.2, pred[128]{0:T(512)(128)(4,1)S(1)} %get-tuple-element.11), kind=kOutput, calls=%fused_computation.7 | convolution fusion | flops 1610616832 | bytes 37749376 | tf_op jit(solution)/shard_map/rt,tif->rif/dot_general | solution.py:34
  151.4 6.6 copy.13
  158.3 10.0 %gather_fusion.1 = bf16[128,256,256]{2,1,0:T(8,128)(2,1)} fusion(bf16[16,256,256]{2,1,0:T(8,128)(2,1)} %bitcast.37, s32[1024]{0:T(1024)S(1)} %pad_clamp_fusion), kind=kCustom, calls=%fused_computation.1 | custom fusion | bytes 33554944 | tf_op jit(solution)/shard_map/gather | solution.py:12
  168.3 21.8 %fusion.29 = f32[128,256,256]{2,1,0:T(8,128)} fusion(bf16[128,256,256]{2,1,0:T(8,128)(2,1)} %gather_fusion.1, bf16[128,256,256]{2,1,0:T(8,128)(2,1)} %param.12), kind=kOutput, calls=%fused_computation.42 | convolution fusion | flops 4294967296 | bytes 67108864 | tf_op jit(solution)/shard_map/tij,tjf->tif/dot_general | solution.py:13
  190.1 34.2 %copy.18 = f32[128,256,256]{1,0,2:T(8,128)} copy(f32[128,256,256]{2,1,0:T(8,128)} %fusion.29) | data formatting | bytes 67108864 | tf_op jit(solution)/shard_map/tij,tjf->tif/dot_general | solution.py:13
  224.3 20.0 %fusion.2 = f32[32,256,256]{2,0,1:T(8,128)} fusion(f32[128,256,256]{1,0,2:T(8,128)} %copy.18, f32[128]{0:T(128)S(1)} %get-tuple-element.12, s32[128]{0:T(128)S(1)} %copy-done.3), kind=kOutput, calls=%fused_computation.5 | convolution fusion | flops 3229618176 | bytes 41944064 | tf_op jit(solution)/shard_map/rt,tif->rif/dot_general | solution.py:17
  244.3 11.5 %copy.14 = f32[32,256,256]{2,1,0:T(8,128)} copy(f32[32,256,256]{2,0,1:T(8,128)} %fusion.2) | data formatting | bytes 16777216 | tf_op jit(solution)/shard_map/rt,tif->rif/dot_general | solution.py:17
  255.9 85.2 %reduce-scatter.6.cloned.1.call-done = f32[512,256]{1,0:T(8,128)} async-done(((f32[8192,256]{1,0:T(8,128)}), f32[512,256]{1,0:T(8,128)}) %reduce-scatter.6.cloned.1.call-update) | async-done | bytes 524304 | tf_op jit(solution)/shard_map/reduce_scatter | solution.py:18
  341.1 2.2 fusion.9
  343.4 51.2 %all-gather.8.cloned.1.call-done = bf16[8192,256]{1,0:T(8,128)(2,1)} async-done(((bf16[512,256]{1,0:T(8,128)(2,1)}), bf16[8192,256]{1,0:T(8,128)(2,1)}) %all-gather.8.cloned.1.call-update) | async-done | bytes 4194320 | tf_op jit(solution)/shard_map/all_gather | solution.py:26
  394.5 10.8 %gather_fusion.2 = bf16[128,256,256]{2,1,0:T(8,128)(2,1)} fusion(bf16[32,256,256]{2,1,0:T(8,128)(2,1)} %bitcast.39, s32[1024]{0:T(1024)S(1)} %pad_clamp_fusion.1), kind=kCustom, calls=%fused_computation.2 | custom fusion | bytes 33554944 | tf_op jit(solution)/shard_map/gather | solution.py:28
  405.4 24.4 %fusion.30 = f32[128,256,256]{2,1,0:T(8,128)} fusion(bf16[128,256,256]{2,1,0:T(8,128)(2,1)} %gather_fusion.2, bf16[128,256,256]{2,1,0:T(8,128)(2,1)} %param.12), kind=kOutput, calls=%fused_computation.43 | convolution fusion | flops 4294967296 | bytes 67108864 | tf_op jit(solution)/shard_map/tji,tjf->tif/dot_general | solution.py:29
  429.8 34.1 %copy.19 = f32[128,256,256]{1,0,2:T(8,128)} copy(f32[128,256,256]{2,1,0:T(8,128)} %fusion.30) | data formatting | bytes 67108864 | tf_op jit(solution)/shard_map/tji,tjf->tif/dot_general | solution.py:29
  463.9 17.6 %fusion = f32[16,256,256]{2,0,1:T(8,128)} fusion(f32[128,256,256]{1,0,2:T(8,128)} %copy.19, s32[128]{0:T(128)S(1)} %copy-done.2, pred[128]{0:T(512)(128)(4,1)S(1)} %get-tuple-element.11), kind=kOutput, calls=%fused_computation.3 | convolution fusion | flops 1610616832 | bytes 37749376 | tf_op jit(solution)/shard_map/rt,tif->rif/dot_general | solution.py:34
  481.6 6.6 copy.15
  489.3 36.5 %reduce-scatter.8.cloned.1.call-done = f32[512,256]{1,0:T(8,128)} async-done(((f32[4096,256]{1,0:T(8,128)}), f32[512,256]{1,0:T(8,128)}) %reduce-scatter.8.cloned.1.call-update) | async-done | bytes 524304 | tf_op jit(solution)/shard_map/reduce_scatter | solution.py:35
  525.9 2.0 convolution_bitcast_fusion
  527.9 2.0 convolution_convert_fusion
  529.9 145.2 %all-reduce.3.cloned.1.call-done = (f32[256,256]{0,1:T(8,128)}, f32[256,256]{1,0:T(8,128)}) async-done(((f32[256,256]{0,1:T(8,128)}, f32[256,256]{1,0:T(8,128)}), (f32[256,256]{0,1:T(8,128)}, f32[256,256]{1,0:T(8,128)})) %all-reduce.3.cloned.1.call-update) | async-done | bytes 524304 | tf_op jit(solution)/shard_map/psum | solution.py:65
  (38 shorter events, 6.6 us)
Async XLA Ops:
  7.2 1.0 copy-start
  7.2 57.1 %all-gather.4.cloned.1.call-start = ((), (), s32[]{:S(2)}) async-start(), calls=%async_computation.3 | async-start | bytes 4456448 | tf_op jit(solution)/shard_map/all_gather | solution.py:26
  7.9 150.4 %all-gather.6.cloned.1.call-start = ((), (), s32[]{:S(2)}) async-start(), calls=%async_computation.5 | async-start | bytes 2359296 | tf_op jit(solution)/shard_map/all_gather | solution.py:10
  10.0 245.9 %reduce-scatter.4.cloned.1.call-start = ((), (), s32[]{:S(2)}) async-start(), calls=%async_computation.4 | async-start | bytes 4718592 | tf_op jit(solution)/shard_map/reduce_scatter | solution.py:35
  99.7 34.1 %copy-start.2 = (s32[128]{0:T(128)S(1)}, s32[128]{0:T(128)}, u32[]{:S(2)}) copy-start(s32[128]{0:T(128)} %param.14) | copy-start | bytes 1540
  158.0 183.1 %reduce-scatter.6.cloned.1.call-start = ((), (), s32[]{:S(2)}) async-start(), calls=%async_computation.6 | async-start | bytes 8912896 | tf_op jit(solution)/shard_map/reduce_scatter | solution.py:18
  190.1 34.2 %copy-start.3 = (s32[128]{0:T(128)S(1)}, s32[128]{0:T(128)}, u32[]{:S(2)}) copy-start(s32[128]{0:T(128)} %param.13) | copy-start | bytes 1540
  244.3 96.8 %copy-start.6 = (bf16[256,256]{1,0:T(8,128)(2,1)S(1)}, bf16[256,256]{1,0:T(8,128)(2,1)}, u32[]{:S(2)}) copy-start(bf16[256,256]{1,0:T(8,128)(2,1)} %param.11) | copy-start | bytes 393220
  255.8 138.7 %all-gather.8.cloned.1.call-start = ((), (), s32[]{:S(2)}) async-start(), calls=%async_computation.7 | async-start | bytes 4456448 | tf_op jit(solution)/shard_map/all_gather | solution.py:26
  343.3 182.5 %reduce-scatter.8.cloned.1.call-start = ((), (), s32[]{:S(2)}) async-start(), calls=%async_computation.8 | async-start | bytes 4718592 | tf_op jit(solution)/shard_map/reduce_scatter | solution.py:35
  463.9 24.3 %copy-start.4 = (f32[512,256]{1,0:T(8,128)S(1)}, f32[512,256]{1,0:T(8,128)}, u32[]{:S(2)}) copy-start(f32[512,256]{1,0:T(8,128)} %reduce-scatter.4.cloned.1.call-done) | copy-start | bytes 1572868
  463.9 24.3 %copy-start.5 = (f32[512,256]{1,0:T(8,128)S(1)}, f32[512,256]{1,0:T(8,128)}, u32[]{:S(2)}) copy-start(f32[512,256]{1,0:T(8,128)} %reduce-scatter.6.cloned.1.call-done) | copy-start | bytes 1572868
  481.6 46.3 %copy-start.1 = (bf16[256,256]{1,0:T(8,128)(2,1)S(1)}, bf16[256,256]{1,0:T(8,128)(2,1)}, u32[]{:S(2)}) copy-start(bf16[256,256]{1,0:T(8,128)(2,1)} %param.10) | copy-start | bytes 393220
  488.2 186.9 %all-reduce.3.cloned.1.call-start = ((), (), s32[]{:S(2)}) async-start(), calls=%async_computation.9 | async-start | bytes 1048576 | tf_op jit(solution)/shard_map/psum | solution.py:65
Sparse Core Ops, SparseCore 0:
  10.2 54.1 all-gather.3
  66.6 24.6 all-gather.5
  158.1 37.4 reduce-scatter.3
  255.9 85.0 reduce-scatter.5
  343.6 50.8 all-gather.7
  488.3 37.4 reduce-scatter.7
  531.4 143.6 all-reduce.2
where the time goes:
time: 689 us; the launch traced here: 685 us
  waiting for transfers between devices  372 us (54%)
  local copies, waits for them, and re-layouts  162 us (24%)
  matrix products  135 us (20%)
  between operations  14.9 us (2%)
    psum x1, waiting for transfers between devices, per_device(): grad_one = lax.psum(grad_one, ('row', 'col'))  145 us
    all_gather x2, waiting for transfers between devices, transposed_product(): gathered = lax.all_gather(shard, 'col', axis=0, tiled=True)  104 us
    reduce_scatter x1, waiting for transfers between devices, forward_product(): lax.psum_scatter(partial_value.reshape(-1, feat_width), 'col', scatter_di...  85.2 us
    dot_general x2, local copies, waits for them, and re-layouts, transposed_product(): jnp.einsum('tji,tjf->tif', tile_values, picked, preferred_element_type=jn...  68.3 us
    dot_general x2, matrix products, transposed_product(): jnp.einsum('tji,tjf->tif', tile_values, picked, preferred_element_type=jn...  49.2 us
    reduce_scatter x2, waiting for transfers between devices, transposed_product(): lax.psum_scatter(partial_value.reshape(-1, feat_width), 'row', scatter_di...  36.6 us
    dot_general x2, matrix products, transposed_product(): jnp.einsum('rt,tif->rif', selector, product, precision=lax.Precision.HIGH...  35.1 us
    dot_general x1, local copies, waits for them, and re-layouts, forward_product(): jnp.einsum('tij,tjf->tif', tile_values, picked, preferred_element_type=jn...  34.2 us
  transfers between devices with their start and end apart: 7, of which 5 were waited for; matrix products, arithmetic and copies ran while one was open for 29% of the time, Pallas kernels for 0%

commit v1 on v0

v1 whole, which is shorter than its diff:
```python
import functools

import jax
import jax.numpy as jnp
from jax import lax
from jax.experimental import pallas as pl
from jax.experimental.pallas import tpu as pltpu
from jax.sharding import PartitionSpec as P

BF = jnp.bfloat16
F32 = jnp.float32
BS = 256
SLOTS = 128
ROW_UNITS = 32
COL_UNITS = 16
UNROLL = 8
WAYS = (1, -1)
DOT = functools.partial(jnp.dot, preferred_element_type=F32)
ROWS_OF_HALF = {1: 0, -1: 1}


class Net:
    def __init__(self, send_sems, recv_sems):
        self.send_sems, self.recv_sems = send_sems, recv_sems
        row, col = lax.axis_index("row"), lax.axis_index("col")
        self.at = {"x": row // 2, "y": col // 4, "z": col % 4}
        self.core = row % 2
        self.keys = {}
        self.started = []

    def off(self, axis, step):
        return (self.at[axis] + (step + 4)) % 4

    def peer(self, axis, step):
        at = dict(self.at)
        core = self.core
        if axis == "core":
            core = 1 - core
        else:
            at[axis] = self.off(axis, step)
        return (at["x"] * 2 + core, at["y"] * 4 + at["z"])

    def greet(self):
        barrier = pltpu.get_barrier_semaphore()
        for axis in ("x", "y", "z"):
            for way in WAYS:
                pl.semaphore_signal(
                    barrier, inc=1, device_id=self.peer(axis, way), device_id_type=pl.DeviceIdType.MESH
                )
        pl.semaphore_signal(
            barrier, inc=1, device_id=self.peer("core", 0), device_id_type=pl.DeviceIdType.MESH
        )

    def met(self):
        pl.semaphore_wait(pltpu.get_barrier_semaphore(), 7)

    def number(self, key):
        return self.keys.setdefault(key, len(self.keys))

    def copy(self, key, src, dst, axis, way):
        at = self.number(key)
        return pltpu.make_async_remote_copy(
            src_ref=src,
            dst_ref=dst,
            send_sem=self.send_sems.at[at],
            recv_sem=self.recv_sems.at[at],
            device_id=self.peer(axis, way),
            device_id_type=pl.DeviceIdType.MESH,
        )

    def send(self, key, src, dst, axis, way):
        copy = self.copy(key, src, dst, axis, way)
        copy.start()
        self.started.append(copy)

    def got(self, key, dst, axis, way):
        self.copy(key, dst, dst, axis, way).wait_recv()

    def drain(self):
        for copy in self.started:
            copy.wait_send()


class GatherPlane:
    def __init__(self, net, tag, buf):
        self.net, self.tag, self.buf = net, tag, buf
        self.half_rows = buf.shape[1] // 2

    def axes(self, block):
        return ("y", "z") if block == 0 else ("z", "y")

    def unit(self, block, first, second):
        one, two = self.axes(block)
        at = {one: self.net.off(one, first), two: self.net.off(two, second)}
        return (at["y"] * 4 + at["z"]) * 2 + block

    def whole(self, block, first, second):
        return self.buf.at[self.unit(block, first, second)]

    def half(self, block, first, second, way):
        rows = pl.ds(ROWS_OF_HALF[way] * self.half_rows, self.half_rows)
        return self.buf.at[self.unit(block, first, second), rows]

    def put(self, key, ref, axis, way):
        self.net.send((self.tag, *key), ref, ref, axis, way)

    def get(self, key, ref, axis, way):
        self.net.got((self.tag, *key), ref, axis, way)

    def spread(self, block, first):
        two = self.axes(block)[1]
        for way in WAYS:
            self.put(("c", block, first, way), self.whole(block, first, 0), two, way)

    def start(self):
        for block in (0, 1):
            one = self.axes(block)[0]
            for way in WAYS:
                self.put(("a", block, way), self.whole(block, 0, 0), one, way)
        for block in (0, 1):
            self.spread(block, 0)

    def step1(self):
        for way in WAYS:
            for block in (0, 1):
                one = self.axes(block)[0]
                self.get(("a", block, way), self.whole(block, -way, 0), one, way)
                self.put(("f", block, way), self.half(block, -way, 0, way), one, way)
                self.spread(block, -way)

    def pass_on(self, first):
        for block in (0, 1):
            two = self.axes(block)[1]
            for way in WAYS:
                self.get(("c", block, first, way), self.whole(block, first, -way), two, way)
                self.put(("e", block, first, way), self.half(block, first, -way, way), two, way)

    def step2(self):
        self.pass_on(0)

    def step3(self):
        for block in (0, 1):
            one = self.axes(block)[0]
            for way in WAYS:
                self.get(("f", block, way), self.half(block, 2, 0, way), one, way)
            self.spread(block, 2)

    def step4(self):
        self.pass_on(-1)
        self.pass_on(1)

    def step5(self):
        self.pass_on(2)

    def finish(self):
        for first in (0, -1, 1, 2):
            for block in (0, 1):
                two = self.axes(block)[1]
                for way in WAYS:
                    self.get(("e", block, first, way), self.half(block, first, 2, way), two, way)


class GatherLine:
    def __init__(self, net, tag, buf):
        self.net, self.tag, self.buf = net, tag, buf

    def first(self, step, core):
        return (self.net.off("x", step) * 2 + core) * 2

    def pair(self, step, other=False):
        core = 1 - self.net.core if other else self.net.core
        return self.buf.at[pl.ds(self.first(step, core), 2)]

    def half(self, step, way):
        return self.buf.at[self.first(step, self.net.core) + ROWS_OF_HALF[way]]

    def share(self, step):
        self.net.send((self.tag, "s", step), self.pair(step), self.pair(step), "core", 0)

    def start(self):
        for way in WAYS:
            self.net.send((self.tag, "a", way), self.pair(0), self.pair(0), "x", way)
        self.share(0)

    def step1(self):
        for way in WAYS:
            self.net.got((self.tag, "a", way), self.pair(-way), "x", way)
            ref = self.half(-way, way)
            self.net.send((self.tag, "f", way), ref, ref, "x", way)
            self.share(-way)

    def step2(self):
        for way in WAYS:
            self.net.got((self.tag, "f", way), self.half(2, way), "x", way)
        self.share(2)

    def finish(self):
        for step in (0, -1, 1, 2):
            self.net.got((self.tag, "s", step), self.pair(step, other=True), "core", 0)


class RingSum:
    def __init__(self, net, tag, axis, half, relay, landed):
        self.net, self.tag, self.axis = net, tag, axis
        self.half, self.relay, self.landed = half, relay, landed

    def start(self):
        for way in WAYS:
            self.net.send(
                (self.tag, "p", way), self.half(2, ROWS_OF_HALF[way]), self.relay[way], self.axis, way
            )

    def start_near(self):
        for way in WAYS:
            rest = 1 - ROWS_OF_HALF[way]
            self.net.send(
                (self.tag, "q", way), self.half(way, rest), self.landed[way][rest], self.axis, way
            )

    def middle(self):
        for way in WAYS:
            turn = ROWS_OF_HALF[way]
            self.net.got((self.tag, "p", way), self.relay[way], self.axis, way)
            mine = self.half(way, turn)
            mine[...] = (mine[...].astype(F32) + self.relay[way][...].astype(F32)).astype(BF)
            self.net.send((self.tag, "r", way), mine, self.landed[way][turn], self.axis, way)

    def finish(self, h, own=None):
        total = (self.half(0, h)[...] if own is None else own).astype(F32)
        for way in WAYS:
            kind = "r" if ROWS_OF_HALF[way] == h else "q"
            self.net.got((self.tag, kind, way), self.landed[way][h], self.axis, way)
            total = total + self.landed[way][h][...].astype(F32)
        return total


class LineSum:
    def __init__(self, net, tag, part, swapped, relay, landed):
        self.net, self.tag, self.part, self.swapped = net, tag, part, swapped
        self.ring = RingSum(
            net,
            (tag, "ring"),
            "x",
            lambda step, h: part.at[self.first(step, net.core) + h],
            {1: relay.at[0], -1: relay.at[1]},
            {1: [landed.at[0], landed.at[1]], -1: [landed.at[2], landed.at[3]]},
        )

    def first(self, step, core):
        return (self.net.off("x", step) * 2 + core) * 2

    def there(self, step):
        return self.swapped.at[pl.ds(self.net.off("x", step) * 2, 2)]

    def start(self):
        for step in (2, 1, -1, 0):
            src = self.part.at[pl.ds(self.first(step, 1 - self.net.core), 2)]
            self.net.send((self.tag, "s", step), src, self.there(step), "core", 0)

    def join(self, step):
        self.net.got((self.tag, "s", step), self.there(step), "core", 0)
        for h in (0, 1):
            mine = self.part.at[self.first(step, self.net.core) + h]
            other = self.swapped.at[self.net.off("x", step) * 2 + h]
            mine[...] = (mine[...].astype(F32) + other[...].astype(F32)).astype(BF)

    def middle(self):
        self.join(2)
        self.ring.start()
        self.join(1)
        self.join(-1)
        self.ring.start_near()
        self.join(0)

    def late(self):
        self.ring.middle()

    def finish(self, h):
        return self.ring.finish(h)


class PlaneSum:
    ORDER = (2, 1, -1, 0)

    def __init__(self, net, tag, part, relay, landed, part2, relay2, landed2):
        self.net, self.part, self.part2 = net, part, part2
        rows = part.shape[1] // 2
        cut = [pl.ds(0, rows), pl.ds(rows, rows)]
        self.cut = cut
        self.rings, self.last = {}, {}
        for block in (0, 1):
            one, two = ("z", "y") if block == 0 else ("y", "z")

            def unit(first, second, block=block, one=one, two=two):
                at = {one: net.off(one, first), two: net.off(two, second)}
                return (at["y"] * 4 + at["z"]) * 2 + block

            for k, second in enumerate(self.ORDER):
                base = (block * 4 + k) * 2
                self.rings[block, k] = RingSum(
                    net,
                    (tag, "one", block, k),
                    one,
                    lambda step, h, unit=unit, second=second: part.at[unit(step, second), cut[h]],
                    {1: relay.at[base], -1: relay.at[base + 1]},
                    {
                        1: [landed.at[base, cut[h]] for h in (0, 1)],
                        -1: [landed.at[base + 1, cut[h]] for h in (0, 1)],
                    },
                )
            base = block * 2
            self.last[block] = RingSum(
                net,
                (tag, "two", block),
                two,
                lambda step, h, block=block: part2.at[block * 4 + self.ORDER.index(step), cut[h]],
                {1: relay2.at[base], -1: relay2.at[base + 1]},
                {
                    1: [landed2.at[base, cut[h]] for h in (0, 1)],
                    -1: [landed2.at[base + 1, cut[h]] for h in (0, 1)],
                },
            )

    def start(self, k):
        for block in (0, 1):
            self.rings[block, k].start()
        for block in (0, 1):
            self.rings[block, k].start_near()

    def middle(self, k):
        for block in (0, 1):
            self.rings[block, k].middle()

    def close(self, k):
        for block in (0, 1):
            for h in (0, 1):
                total = self.rings[block, k].finish(h)
                self.part2[block * 4 + k, self.cut[h]] = total.astype(BF)
        if k == 0:
            for block in (0, 1):
                self.last[block].start()
        if k == 2:
            for block in (0, 1):
                self.last[block].start_near()

    def late(self):
        for block in (0, 1):
            self.last[block].middle()

    def finish(self, block, h):
        return self.last[block].finish(h)


def products(count, begin, left, right, keep, total, sums):
    def body(step, carry):
        for turn in range(UNROLL):
            t = begin + step * UNROLL + turn
            value = total[...] * keep(t) + DOT(left(t), right(t))
            total[...] = value
            sums[t] = value.astype(BF)
        return carry

    lax.fori_loop(0, count // UNROLL, body, 0)


def pick(units, sums, last, some, part):
    def body(u, carry):
        part[u] = (sums[last(u)].astype(F32) * some(u)).astype(BF)
        return carry

    lax.fori_loop(0, units, body, 0)


def both(values):
    high = values.astype(BF)
    return high, (values - high.astype(F32)).astype(BF)


NT = (((1,), (1,)), ((), ()))


def front_kernel(
    plan, feats, cot, w_one, w_two, tiles_hbm, grad_pre, grad_one, grad_two,
    tiles, sums, total, feats_all, cot_all, part, relay, landed, part2, relay2, landed2,
    part_x, swapped, relay_x, landed_x, w_one_t, tile_sem, send_sems, recv_sems,
):
    net = Net(send_sems, recv_sems)
    net.greet()
    load = pltpu.make_async_copy(tiles_hbm, tiles, tile_sem)
    load.start()
    line = GatherLine(net, "x", feats_all)
    plane = GatherPlane(net, "g", cot_all)
    for block in (0, 1):
        rows = pl.ds(block * BS, BS)
        feats_all[line.first(0, net.core) + block] = feats[rows]
        cot_all[plane.unit(block, 0, 0)] = cot[rows].astype(F32).T.astype(BF)
    net.met()
    line.start()
    plane.start()
    w_one_t[...] = w_one[...].astype(F32).T.astype(BF)
    total[...] = jnp.zeros_like(total)
    line.step1()
    plane.step1()
    line.step2()
    plane.step2()
    plane.step3()
    line.finish()
    load.wait()

    def ahead(count, begin):
        products(
            count,
            begin,
            lambda t: tiles[plan[0, t]],
            lambda t: feats_all[plan[1, t]],
            lambda t: plan[2, t].astype(F32),
            total,
            sums,
        )

    ahead(64, 0)
    plane.step4()
    ahead(64, 64)
    plane.step5()
    pick(ROW_UNITS, sums, lambda u: plan[6, u], lambda u: plan[6, u + 32].astype(F32), part)
    plane_sum = PlaneSum(net, "ax", part, relay, landed, part2, relay2, landed2)
    for k in range(4):
        plane_sum.start(k)
    plane.finish()
    total[...] = jnp.zeros_like(total)
    products(
        SLOTS,
        0,
        lambda t: cot_all[plan[4, t]],
        lambda t: tiles[plan[3, t]],
        lambda t: plan[5, t].astype(F32),
        total,
        sums,
    )
    pick(COL_UNITS, sums, lambda u: plan[6, u + 64], lambda u: plan[6, u + 96].astype(F32), part_x)
    line_sum = LineSum(net, "bt", part_x, swapped, relay_x, landed_x)
    line_sum.start()
    plane_sum.middle(0)
    plane_sum.middle(1)
    plane_sum.middle(2)
    plane_sum.middle(3)
    line_sum.middle()
    plane_sum.close(0)
    line_sum.late()
    plane_sum.close(1)
    plane_sum.close(2)
    plane_sum.close(3)
    plane_sum.late()
    back = [line_sum.finish(block).astype(BF) for block in (0, 1)]
    d_hidden = [DOT(w_two[...], back[block]) for block in (0, 1)]
    one = jnp.zeros((BS, BS), F32)
    two = jnp.zeros((BS, BS), F32)
    for block in (0, 1):
        ax = jnp.concatenate([plane_sum.finish(block, h) for h in (0, 1)], axis=0).T
        high, low = both(ax)
        pre = DOT(w_one_t[...], high) + DOT(w_one_t[...], low)
        gate = 1.0 / (1.0 + jnp.exp(-pre))
        hidden = (pre * gate).astype(BF)
        slope = (d_hidden[block] * gate * (1.0 + pre * (1.0 - gate))).astype(BF)
        grad_pre[block] = slope
        two += lax.dot_general(hidden, back[block], NT, preferred_element_type=F32)
        one += lax.dot_general(high, slope, NT, preferred_element_type=F32)
        one += lax.dot_general(low, slope, NT, preferred_element_type=F32)
    grad_one[...] = one
    grad_two[...] = two
    net.drain()


def back_kernel(
    plan, grad_pre, w_one, tiles_hbm, input_grad,
    tiles, sums, total, grad_all_0, grad_all_1, part_0, swapped_0, relay_0, landed_0,
    part_1, swapped_1, relay_1, landed_1, result, tile_sem, send_sems, recv_sems,
):
    net = Net(send_sems, recv_sems)
    net.greet()
    load = pltpu.make_async_copy(tiles_hbm, tiles, tile_sem)
    load.start()
    half = BS // 2
    gathers, scatters = [], []
    for h, (buf, *scratch) in enumerate(
        (
            (grad_all_0, part_0, swapped_0, relay_0, landed_0),
            (grad_all_1, part_1, swapped_1, relay_1, landed_1),
        )
    ):
        gathers.append(GatherPlane(net, ("p", h), buf))
        scatters.append(LineSum(net, ("s", h), *scratch))
        for block in (0, 1):
            buf[gathers[h].unit(block, 0, 0)] = grad_pre[block, pl.ds(h * half, half)]
    net.met()
    total[...] = jnp.zeros_like(total)
    early, late = gathers
    early.start()
    early.step1()
    early.step2()
    early.step3()
    early.step4()
    late.start()
    early.step5()
    late.step1()
    late.step2()
    early.finish()
    load.wait()

    def run(count, begin, buf):
        products(
            count,
            begin,
            lambda t: buf[plan[4, t]],
            lambda t: tiles[plan[3, t]],
            lambda t: plan[5, t].astype(F32),
            total,
            sums,
        )

    def choose(part):
        pick(COL_UNITS, sums, lambda u: plan[6, u + 64], lambda u: plan[6, u + 96].astype(F32), part)

    def apply(h):
        for block in (0, 1):
            back = scatters[h].finish(block).astype(BF)
            value = DOT(w_one[:, h * half : (h + 1) * half], back)
            if h == 0:
                result[block] = value
            else:
                input_grad[pl.ds(block * BS, BS)] = (result[block] + value).T.astype(BF)

    run(64, 0, grad_all_0)
    late.step3()
    run(64, 64, grad_all_0)
    late.step4()
    choose(part_0)
    scatters[0].start()
    late.step5()
    scatters[0].middle()
    scatters[0].late()
    apply(0)
    late.finish()
    total[...] = jnp.zeros_like(total)
    run(SLOTS, 0, grad_all_1)
    choose(part_1)
    scatters[1].start()
    scatters[1].middle()
    scatters[1].late()
    apply(1)
    net.drain()


def in_order(major, minor, live):
    slots = jnp.arange(SLOTS, dtype=jnp.int32)
    key = jnp.where(live, major * 64 + minor, 4096 + slots)
    rank = jnp.sum((key[None, :] < key[:, None]).astype(jnp.int32), axis=1)
    at = rank[:, None] == slots[None, :]
    order = jnp.sum(jnp.where(at, slots[:, None], 0), axis=0)
    minors = jnp.sum(jnp.where(at, minor[:, None], 0), axis=0)
    majors = jnp.sum(jnp.where(at, jnp.where(live, major, -1)[:, None], 0), axis=0)
    keep = jnp.concatenate([jnp.zeros((1,), jnp.int32), (majors[1:] == majors[:-1]).astype(jnp.int32)])
    return order, minors, keep


def ends(major, live, units):
    unit = jnp.arange(units, dtype=jnp.int32)[:, None]
    before = jnp.sum(((major[None, :] <= unit) & live[None, :]).astype(jnp.int32), axis=1)
    some = jnp.any((major[None, :] == unit) & live[None, :], axis=1)
    pad = jnp.zeros((32 - units,), jnp.int32)
    return [jnp.maximum(before - 1, 0), pad, some.astype(jnp.int32), pad]


def make_plan(tile_rows, tile_cols, tile_count):
    live = jnp.arange(SLOTS, dtype=jnp.int32) < tile_count[0]
    rows, cols = jnp.clip(tile_rows, 0, ROW_UNITS - 1), jnp.clip(tile_cols, 0, COL_UNITS - 1)
    last = jnp.concatenate(ends(rows, live, ROW_UNITS) + ends(cols, live, COL_UNITS))
    none = jnp.zeros((SLOTS,), jnp.int32)
    return jnp.stack([*in_order(rows, cols, live), *in_order(cols, rows, live), last, none])


def units(count, rows=BS):
    return pltpu.VMEM((count, rows, BS), BF)


SMEM = pl.BlockSpec(memory_space=pltpu.SMEM)
VMEM = pl.BlockSpec(memory_space=pltpu.VMEM)
ANY = pl.BlockSpec(memory_space=pl.ANY)


def front(plan, feats, cot, w_one, w_two, tiles):
    half = BS // 2
    return pl.pallas_call(
        front_kernel,
        out_shape=(
            jax.ShapeDtypeStruct((2, BS, BS), BF),
            jax.ShapeDtypeStruct((BS, BS), F32),
            jax.ShapeDtypeStruct((BS, BS), F32),
        ),
        in_specs=[SMEM, VMEM, VMEM, VMEM, VMEM, ANY],
        out_specs=(VMEM, VMEM, VMEM),
        scratch_shapes=[
            units(SLOTS),
            units(SLOTS),
            pltpu.VMEM((BS, BS), F32),
            units(COL_UNITS),
            units(ROW_UNITS),
            units(ROW_UNITS),
            units(16, half),
            units(16),
            units(8),
            units(4, half),
            units(4),
            units(COL_UNITS),
            units(8),
            units(2),
            units(4),
            pltpu.VMEM((BS, BS), BF),
            pltpu.SemaphoreType.DMA,
            pltpu.SemaphoreType.DMA((120,)),
            pltpu.SemaphoreType.DMA((120,)),
        ],
        compiler_params=pltpu.CompilerParams(
            collective_id=0, has_side_effects=True, vmem_limit_bytes=60 * 2**20
        ),
        name="front",
    )(plan, feats, cot, w_one, w_two, tiles)


def back(plan, grad_pre, w_one, tiles):
    half = BS // 2
    sums = [units(COL_UNITS, half), units(8, half), units(2, half), units(4, half)]
    return pl.pallas_call(
        back_kernel,
        out_shape=jax.ShapeDtypeStruct((2 * BS, BS), BF),
        in_specs=[SMEM, VMEM, VMEM, ANY],
        out_specs=VMEM,
        scratch_shapes=[
            units(SLOTS),
            units(SLOTS, half),
            pltpu.VMEM((half, BS), F32),
            units(ROW_UNITS, half),
            units(ROW_UNITS, half),
            *sums,
            *sums,
            pltpu.VMEM((2, BS, BS), F32),
            pltpu.SemaphoreType.DMA,
            pltpu.SemaphoreType.DMA((120,)),
            pltpu.SemaphoreType.DMA((120,)),
        ],
        compiler_params=pltpu.CompilerParams(
            collective_id=1, has_side_effects=True, vmem_limit_bytes=60 * 2**20
        ),
        name="back",
    )(plan, grad_pre, w_one, tiles)


def per_device(
    node_feats, out_grad, weight_one, weight_two, tile_values, tile_rows, tile_cols, tile_count
):
    plan = make_plan(tile_rows, tile_cols, tile_count)
    grad_pre, grad_one, grad_two = front(plan, node_feats, out_grad, weight_one, weight_two, tile_values)
    grads = lax.psum(jnp.concatenate([grad_one, grad_two], axis=0), ("row", "col"))
    input_grad = back(plan, grad_pre, weight_one, tile_values)
    return (input_grad, grads[:BS], grads[BS:])


def solution(mesh):
    in_specs = (
        P(("row", "col"), None),
        P(("row", "col"), None),
        P(),
        P(),
        P(("row", "col"), None, None),
        P(("row", "col")),
        P(("row", "col")),
        P(("row", "col")),
    )
    out_specs = (P(("row", "col"), None), P(), P())
    return jax.shard_map(
        per_device, mesh=mesh, in_specs=in_specs, out_specs=out_specs, check_vma=False
    )
```

time: 689 us -> 231 us (0.34)
  waiting for transfers between devices: 372 us -> 90.4 us
  local copies, waits for them, and re-layouts: 162 us -> 4.22 us
  matrix products: 135 us -> 0 us
  Pallas kernels: 0 us -> 116 us
    dot_general x11 -> x0, matrix products: 135 us -> none  [the longest x2 49.2 us: transposed_product(): jnp.einsum('tji,tjf->tif', tile_values, picked, preferred_element_type=jn...]
    dot_general x6 -> x0, local copies, waits for them, and re-layouts: 127 us -> none  [the longest x2 68.3 us: transposed_product(): jnp.einsum('tji,tjf->tif', tile_values, picked, preferred_element_type=jn...]
    reduce_scatter x3 -> x0, waiting for transfers between devices: 122 us -> none  [the longest x1 85.2 us: forward_product(): lax.psum_scatter(partial_value.reshape(-1, feat_width), 'col', scatter_di...]
    pallas_call x0 -> x2, Pallas kernels: none -> 116 us  [the longest x1 61.8 us: front(): pl.pallas_call(front_kernel, out_shape=(jax.ShapeDtypeStruct((2, BS, BS),...]
    all_gather x3 -> x0, waiting for transfers between devices: 104 us -> none  [the longest x2 104 us: transposed_product(): gathered = lax.all_gather(shard, 'col', axis=0, tiled=True)]
    psum x1, waiting for transfers between devices: 145 us -> 90.4 us  [per_device(): lax.psum(jnp.concatenate([grad_one, grad_two], axis=0), ('row', 'col'))]
    gather x3 -> x0, local copies, waits for them, and re-layouts: 31.5 us -> none  [the longest x2 21.5 us: transposed_product(): picked = blocks[tile_rows]]
  transfers between devices with their start and end apart: 7 -> 1, of which waited for: 5 -> 1; matrix products, arithmetic and copies ran while one was open for 29% -> 0% of each run, Pallas kernels for 0% -> 24%
where the time goes in v1:
time: 231 us; the launch traced here: 229 us
  Pallas kernels  116 us (50%)
  waiting for transfers between devices  90.4 us (39%)
  between operations  14.8 us (6%)
  local copies, waits for them, and re-layouts  4.22 us (2%)
  other arithmetic  3.86 us (2%)
    psum x1, waiting for transfers between devices, per_device(): lax.psum(jnp.concatenate([grad_one, grad_two], axis=0), ('row', 'col'))  90.4 us
    pallas_call x1, Pallas kernels, front(): pl.pallas_call(front_kernel, out_shape=(jax.ShapeDtypeStruct((2, BS, BS),...  61.8 us
    pallas_call x1, Pallas kernels, back(): pl.pallas_call(back_kernel, out_shape=jax.ShapeDtypeStruct((2 * BS, BS),...  53.9 us
  transfers between devices with their start and end apart: 1, of which 1 were waited for; matrix products, arithmetic and copies ran while one was open for 0% of the time, Pallas kernels for 24%

profile of v1, /device:TPU:0, one launch (start us, length us, event | category | flops | bytes accessed | tf_op | source)
XLA Modules:
  0.0 229.0 jit_solution(1258843261745993263)
XLA Ops:
  7.2 0.0 all-reduce.2.cloned.1.call-start
  7.9 0.7 broadcast_clamp_fusion.1
  8.6 0.1 fusion.2
  8.7 0.1 convert_reduce_fusion.2
  8.8 0.1 convert_reduce_fusion.3
  8.9 0.1 fusion.5
  9.0 0.2 convert_reduce_fusion.1
  9.2 0.2 convert_reduce_fusion
  9.4 0.2 select_reduce_fusion
  9.6 0.1 slice_compare_fusion
  9.7 0.1 slice_compare_fusion.1
  9.8 0.1 fusion.8
  9.8 0.1 fusion.9
  9.9 0.1 concatenate.16
  10.0 0.6 stack.39.plan
  10.6 61.8 %front.1 = (bf16[2,256,256]{2,1,0:T(8,128)(2,1)}, f32[256,256]{1,0:T(8,128)}, f32[256,256]{1,0:T(8,128)}) custom-call(s32[8,128]{1,0:T(8,128)} %stack.39.plan, bf16[512,256]{1,0:T(8,128)(2,1)} %feats.1, bf16[512,256]{1,0:T(8,128)(2,1)} %cot.1, bf16[256,256]{1,0:T(8,128)(2,1)} %w_one.3, bf16[256,256]{1,0:T(8,128)(2,1)} %w_two.1, bf16[128,256,256]{2,1,0:T(8,128)(2,1)} %tiles_hbm.3), custom_call_target="tpu_custom_call" | custom-call | tf_op jit(solution)/shard_map/front/pallas_call | solution.py:593
  72.5 1.9 pad_maximum_fusion
  74.3 0.0 all-reduce.2.cloned.1.call-update
  74.3 53.9 %back.1 = bf16[512,256]{1,0:T(8,128)(2,1)} custom-call(s32[8,128]{1,0:T(8,128)} %stack.39.plan, bf16[2,256,256]{2,1,0:T(8,128)(2,1)} %get-tuple-element.6.grad_pre, bf16[256,256]{1,0:T(8,128)(2,1)} %w_one.3, bf16[128,256,256]{2,1,0:T(8,128)(2,1)} %tiles_hbm.3), custom_call_target="tpu_custom_call" | custom-call | tf_op jit(solution)/shard_map/back/pallas_call | solution.py:633
  128.2 90.4 %all-reduce.2.cloned.1.call-done = f32[512,256]{1,0:T(8,128)} async-done(((f32[512,256]{1,0:T(8,128)}), f32[512,256]{1,0:T(8,128)}) %all-reduce.2.cloned.1.call-update) | async-done | bytes 524304 | tf_op jit(solution)/shard_map/psum | solution.py:663
  218.6 1.9 fusion.11
  220.5 1.7 copy.14
  (7 shorter events, 0.0 us)
Async XLA Ops:
  7.2 211.4 %all-reduce.2.cloned.1.call-start = ((), (), s32[]{:S(2)}) async-start(), calls=%async_computation | async-start | bytes 1048576 | tf_op jit(solution)/shard_map/psum | solution.py:663
Sparse Core Ops, SparseCore 0:
  74.4 144.1 all-reduce.1

commit v2 on v1

v2 whole, which is shorter than its diff:
```python
import functools

import jax
import jax.numpy as jnp
from jax import lax
from jax.experimental import pallas as pl
from jax.experimental.pallas import tpu as pltpu
from jax.sharding import PartitionSpec as P

BF = jnp.bfloat16
F32 = jnp.float32
BS = 256
SLOTS = 128
ROW_UNITS = 32
COL_UNITS = 16
UNROLL = 16
WAYS = (1, -1)
DOT = functools.partial(jnp.dot, preferred_element_type=F32)
ROWS_OF_HALF = {1: 0, -1: 1}
PARTNERS = [(axis, step) for axis in ("x", "y", "z") for step in (1, -1, 2)] + [("core", 0)]


class Net:
    def __init__(self, sems):
        self.sems = sems
        row, col = lax.axis_index("row"), lax.axis_index("col")
        self.at = {"x": row // 2, "y": col // 4, "z": col % 4}
        self.core = row % 2
        self.keys = {}

    def off(self, axis, step):
        return (self.at[axis] + (step + 4)) % 4

    def peer(self, axis, step):
        at = dict(self.at)
        core = self.core
        if axis == "core":
            core = 1 - core
        else:
            at[axis] = self.off(axis, step)
        return (at["x"] * 2 + core, at["y"] * 4 + at["z"])

    def greet(self):
        barrier = pltpu.get_barrier_semaphore()
        for axis, way in PARTNERS:
            pl.semaphore_signal(
                barrier, inc=1, device_id=self.peer(axis, way), device_id_type=pl.DeviceIdType.MESH
            )

    def met(self):
        pl.semaphore_wait(pltpu.get_barrier_semaphore(), len(PARTNERS))

    def copy(self, leave, land, src, dst, axis, way):
        at = [self.keys.setdefault(key, len(self.keys)) for key in (("out", leave), ("in", land))]
        return pltpu.make_async_remote_copy(
            src_ref=src,
            dst_ref=dst,
            send_sem=self.sems.at[at[0]],
            recv_sem=self.sems.at[at[1]],
            device_id=self.peer(axis, way),
            device_id_type=pl.DeviceIdType.MESH,
        )

    def send(self, leave, land, src, dst, axis, way):
        self.copy(leave, land, src, dst, axis, way).start()

    def got(self, leave, land, ref):
        self.copy(leave, land, ref, ref, "core", 0).wait_recv()

    def left(self, leave, land, ref):
        self.copy(leave, land, ref, ref, "core", 0).wait_send()


class GatherPlane:
    def __init__(self, net, tag, buf):
        self.net, self.tag, self.buf = net, tag, buf
        self.half_rows = buf.shape[1] // 2

    def axes(self, block):
        return ("y", "z") if block == 0 else ("z", "y")

    def unit(self, block, first, second):
        one, two = self.axes(block)
        at = {one: self.net.off(one, first), two: self.net.off(two, second)}
        return (at["y"] * 4 + at["z"]) * 2 + block

    def whole(self, block, first, second):
        return self.buf.at[self.unit(block, first, second)]

    def half(self, block, first, second, way):
        rows = pl.ds(ROWS_OF_HALF[way] * self.half_rows, self.half_rows)
        return self.buf.at[self.unit(block, first, second), rows]

    def put(self, key, ref, axis, way):
        self.net.send(self.tag, (self.tag, *key), ref, ref, axis, way)

    def get(self, key, count):
        self.net.got(self.tag, (self.tag, *key), self.buf.at[pl.ds(0, count)])

    def spread(self, block, first):
        two = self.axes(block)[1]
        for way in WAYS:
            self.put(("c", first), self.whole(block, first, 0), two, way)

    def start(self):
        for block in (0, 1):
            one = self.axes(block)[0]
            for way in WAYS:
                self.put(("a",), self.whole(block, 0, 0), one, way)

    def start_more(self):
        for block in (0, 1):
            self.spread(block, 0)

    def step1(self):
        self.get(("a",), 4)
        for block in (0, 1):
            one = self.axes(block)[0]
            for way in WAYS:
                self.put(("f",), self.half(block, -way, 0, way), one, way)
        for way in WAYS:
            for block in (0, 1):
                self.spread(block, -way)

    def pass_on(self, first):
        self.get(("c", first), 4)
        for block in (0, 1):
            two = self.axes(block)[1]
            for way in WAYS:
                self.put(("e",), self.half(block, first, -way, way), two, way)

    def step2(self):
        self.pass_on(0)

    def step3(self):
        self.get(("f",), 2)
        for block in (0, 1):
            self.spread(block, 2)

    def step4(self):
        self.pass_on(-1)
        self.pass_on(1)

    def step5(self):
        self.pass_on(2)

    def finish(self):
        self.get(("e",), 8)

    def left(self):
        self.net.left(self.tag, (self.tag, "a"), self.buf.at[pl.ds(0, 30)])


class GatherLine:
    def __init__(self, net, tag, buf):
        self.net, self.tag, self.buf = net, tag, buf

    def first(self, step, core):
        return (self.net.off("x", step) * 2 + core) * 2

    def get(self, kind, count):
        self.net.got(self.tag, (self.tag, kind), self.buf.at[pl.ds(0, count)])

    def share(self, step):
        ref = self.buf.at[pl.ds(self.first(step, self.net.core), 2)]
        self.net.send(self.tag, (self.tag, "s"), ref, ref, "core", 0)

    def pass_half(self, kind, step, h, way):
        ref = self.buf.at[self.first(step, self.net.core) + h]
        self.net.send(self.tag, (self.tag, kind), ref, ref, "x", way)

    def start(self):
        for way in WAYS:
            self.pass_half("a", 0, ROWS_OF_HALF[way], way)

    def start_more(self):
        for way in WAYS:
            self.pass_half("b", 0, 1 - ROWS_OF_HALF[way], way)
        self.share(0)

    def step1(self):
        self.get("a", 2)
        for way in WAYS:
            self.pass_half("f", -way, ROWS_OF_HALF[way], way)

    def step2(self):
        self.get("b", 2)
        for way in WAYS:
            self.share(-way)

    def step3(self):
        self.get("f", 2)
        self.share(2)

    def finish(self):
        self.get("s", 8)

    def left(self):
        self.net.left(self.tag, (self.tag, "a"), self.buf.at[pl.ds(0, 14)])


class RingSum:
    def __init__(self, net, tag, keys, axis, half, relay, landed, more=None):
        self.net, self.tag, self.keys, self.axis = net, tag, keys, axis
        self.half, self.relay, self.landed, self.more = half, relay, landed, more

    def send(self, at, src, dst, way):
        self.net.send(self.tag, self.keys[at], src, dst, self.axis, way)

    def term(self, step, h):
        value = self.half(step, h)[...].astype(F32)
        return value if self.more is None else value + self.more(step, h)[...].astype(F32)

    def start(self):
        for way in WAYS:
            self.send(0, self.half(2, ROWS_OF_HALF[way]), self.relay[way], way)

    def start_near(self):
        for way in WAYS:
            rest = 1 - ROWS_OF_HALF[way]
            self.send(1, self.half(way, rest), self.landed[way][rest], way)

    def middle(self):
        for way in WAYS:
            turn = ROWS_OF_HALF[way]
            mine = self.half(way, turn)
            mine[...] = (self.term(way, turn) + self.relay[way][...].astype(F32)).astype(BF)
            self.send(1, mine, self.landed[way][turn], way)

    def finish(self, h):
        total = self.term(0, h)
        for way in WAYS:
            total = total + self.landed[way][h][...].astype(F32)
        return total


class LineSum:
    def __init__(self, net, tag, part, swapped, relay, landed):
        self.net, self.tag, self.part, self.swapped = net, tag, part, swapped
        self.relay, self.landed = relay, landed
        self.ring = RingSum(
            net,
            tag,
            ((tag, "p"), (tag, "n")),
            "x",
            lambda step, h: part.at[self.first(step, net.core) + h],
            {1: relay.at[0], -1: relay.at[1]},
            {1: [landed.at[0], landed.at[1]], -1: [landed.at[2], landed.at[3]]},
            lambda step, h: swapped.at[net.off("x", step) * 2 + h],
        )

    def first(self, step, core):
        return (self.net.off("x", step) * 2 + core) * 2

    def get(self, kind, ref):
        self.net.got(self.tag, (self.tag, kind), ref)

    def start(self):
        for step in (2, 1, -1, 0):
            src = self.part.at[pl.ds(self.first(step, 1 - self.net.core), 2)]
            dst = self.swapped.at[pl.ds(self.net.off("x", step) * 2, 2)]
            self.net.send(self.tag, (self.tag, "s" if step == 2 else "u"), src, dst, "core", 0)

    def join(self, step, h):
        self.part[self.first(step, self.net.core) + h] = self.ring.term(step, h).astype(BF)

    def middle(self):
        self.get("s", self.swapped.at[pl.ds(0, 2)])
        self.join(2, 0)
        self.join(2, 1)
        self.ring.start()

    def middle_more(self):
        self.get("u", self.swapped.at[pl.ds(0, 6)])
        for way in WAYS:
            self.join(way, 1 - ROWS_OF_HALF[way])
        self.ring.start_near()

    def late(self):
        self.get("p", self.relay)
        self.ring.middle()

    def arrive(self):
        self.get("n", self.landed)

    def finish(self, h):
        return self.ring.finish(h)

    def left(self):
        self.net.left(self.tag, (self.tag, "s"), self.part.at[pl.ds(0, 14)])


class PlaneSum:
    ORDER = (2, 1, -1, 0)

    def __init__(self, net, tag, part, relay, landed, part2, relay2, landed2):
        self.net, self.tag, self.part, self.part2 = net, tag, part, part2
        rows = part.shape[1] // 2
        cut = [pl.ds(0, rows), pl.ds(rows, rows)]
        self.cut = cut
        self.rings, self.last = {}, {}
        for block in (0, 1):
            one, two = ("z", "y") if block == 0 else ("y", "z")

            def unit(first, second, block=block, one=one, two=two):
                at = {one: net.off(one, first), two: net.off(two, second)}
                return (at["y"] * 4 + at["z"]) * 2 + block

            for k, second in enumerate(self.ORDER):
                base = (block * 4 + k) * 2
                self.rings[block, k] = RingSum(
                    net,
                    tag,
                    ((tag, "p", k), (tag, "n", k)),
                    one,
                    lambda step, h, unit=unit, second=second: part.at[unit(step, second), cut[h]],
                    {1: relay.at[base], -1: relay.at[base + 1]},
                    {
                        1: [landed.at[base, cut[h]] for h in (0, 1)],
                        -1: [landed.at[base + 1, cut[h]] for h in (0, 1)],
                    },
                )
            base = block * 2
            self.last[block] = RingSum(
                net,
                tag,
                ((tag, "p", 4), (tag, "n", 4)),
                two,
                lambda step, h, block=block: part2.at[block * 4 + self.ORDER.index(step), cut[h]],
                {1: relay2.at[base], -1: relay2.at[base + 1]},
                {
                    1: [landed2.at[base, cut[h]] for h in (0, 1)],
                    -1: [landed2.at[base + 1, cut[h]] for h in (0, 1)],
                },
            )

    def get(self, kind, k, count):
        self.net.got(self.tag, (self.tag, kind, k), self.part.at[pl.ds(0, count)])

    def start(self, k):
        for block in (0, 1):
            self.rings[block, k].start()

    def start_near(self, k):
        for block in (0, 1):
            self.rings[block, k].start_near()

    def middle(self, k):
        self.get("p", k, 2)
        for block in (0, 1):
            self.rings[block, k].middle()

    def close(self, k):
        self.get("n", k, 4)
        for block in (0, 1):
            for h in (0, 1):
                self.part2[block * 4 + k, self.cut[h]] = self.rings[block, k].finish(h).astype(BF)
        if k == 0:
            for block in (0, 1):
                self.last[block].start()
        if k == 2:
            for block in (0, 1):
                self.last[block].start_near()

    def late(self):
        self.get("p", 4, 2)
        for block in (0, 1):
            self.last[block].middle()

    def arrive(self):
        self.get("n", 4, 4)

    def finish(self, block, h):
        return self.last[block].finish(h)

    def left(self):
        self.net.left(self.tag, (self.tag, "p", 0), self.part.at[pl.ds(0, 30)])


class GradSum:
    FAR = (1, -1, 2)

    def __init__(self, net, mine, swapped, from_x, from_y, from_z, done):
        self.net, self.mine, self.swapped, self.done = net, mine, swapped, done
        self.from_x, self.from_y, self.from_z = from_x, from_y, from_z

    def rows(self, *steps):
        size = {1: 256, 2: 64, 3: 16}[len(steps)]
        at = ((1 - self.net.core) if steps[0] else self.net.core) * 256
        for axis, step, span in zip(("x", "y"), steps[1:], (64, 16)):
            at = at + self.net.off(axis, step) * span
        return pl.ds(pl.multiple_of(at, size), size)

    def put(self, stage, src, dst, axis, step):
        self.net.send(("w", axis), ("w", stage), src, dst, axis, step)

    def get(self, stage, ref):
        self.net.got(("w", "core"), ("w", stage), ref)

    def start(self):
        self.put(0, self.mine.at[self.rows(1)], self.swapped, "core", 0)

    def step1(self):
        self.get(0, self.swapped)
        rows = self.rows(0)
        self.mine[rows] = self.mine[rows] + self.swapped[...]
        for k, step in enumerate(self.FAR):
            self.put(1, self.mine.at[self.rows(0, step)], self.from_x.at[k], "x", step)

    def step2(self):
        self.get(1, self.from_x)
        rows = self.rows(0, 0)
        self.mine[rows] = (self.mine[rows] + self.from_x[0]) + (self.from_x[1] + self.from_x[2])
        for k, step in enumerate(self.FAR):
            self.put(2, self.mine.at[self.rows(0, 0, step)], self.from_y.at[k], "y", step)

    def step3(self):
        self.get(2, self.from_y)
        ref = self.from_z.at[self.net.at["z"]]
        ref[...] = (self.mine[self.rows(0, 0, 0)] + self.from_y[0]) + (self.from_y[1] + self.from_y[2])
        for step in self.FAR:
            self.put(3, ref, ref, "z", step)

    def step4(self):
        self.get(3, self.from_z.at[pl.ds(0, 3)])
        ref = self.done.at[self.rows(0, 0, 0)]
        ref[...] = (self.from_z[0] + self.from_z[1]) + (self.from_z[2] + self.from_z[3])
        for step in self.FAR:
            self.put(4, ref, ref, "y", step)

    def step5(self):
        self.get(4, self.done.at[pl.ds(0, 48)])
        ref = self.done.at[self.rows(0, 0)]
        for step in self.FAR:
            self.put(5, ref, ref, "x", step)

    def step6(self):
        self.get(5, self.done.at[pl.ds(0, 192)])
        ref = self.done.at[self.rows(0)]
        self.put(6, ref, ref, "core", 0)

    def finish(self):
        self.get(6, self.swapped)

    def left(self):
        for axis, rows in (("core", 512), ("x", 384), ("y", 96), ("z", 48)):
            self.net.left(("w", axis), ("w", 0), self.done.at[pl.ds(0, rows)])


def within(index, count):
    return jnp.clip(index, 0, count - 1)


def products(count, begin, left, right, keep, total, sums):
    def body(step, carry):
        for turn in range(UNROLL):
            t = begin + step * UNROLL + turn
            value = total[...] * keep(t) + DOT(left(t), right(t))
            total[...] = value
            sums[t] = value.astype(BF)
        return carry

    lax.fori_loop(0, count // UNROLL, body, 0)


def pick(units, sums, last, some, part):
    def body(u, carry):
        part[u] = (sums[last(u)].astype(F32) * some(u)).astype(BF)
        return carry

    lax.fori_loop(0, units, body, 0)


def both(values):
    high = values.astype(BF)
    return high, (values - high.astype(F32)).astype(BF)


NT = (((1,), (1,)), ((), ()))


def kernel(
    rows, cols, count, feats, cot, w_one, w_two, tiles_hbm, back_out, grads_out,
    plan, plan_wide, tiles, sums, total, feats_all, cot_all, part, relay, landed, part2, relay2, landed2,
    part_x, swapped, relay_x, landed_x, w_one_t,
    slope_all_0, swapped_0, relay_0, landed_0,
    slope_all_1, swapped_1, relay_1, landed_1,
    mine, swapped_w, from_x, from_y, from_z, done, tile_sem, plan_sem, sems,
):
    net = Net(sems)
    net.greet()
    load = pltpu.make_async_copy(tiles_hbm, tiles, tile_sem)
    load.start()
    line = GatherLine(net, "x", feats_all)
    plane = GatherPlane(net, "g", cot_all)
    for block in (0, 1):
        span = pl.ds(block * BS, BS)
        feats_all[line.first(0, net.core) + block] = feats[span]
        cot_all[plane.unit(block, 0, 0)] = cot[span].astype(F32).T.astype(BF)
    net.met()
    line.start()
    plane.start()
    write_plan(rows, cols, count[0], plan_wide)
    to_plan = pltpu.make_async_copy(plan_wide, plan, plan_sem)
    to_plan.start()
    w_one_t[...] = w_one[...].astype(F32).T.astype(BF)
    total[...] = jnp.zeros_like(total)
    line.start_more()
    plane.start_more()
    line.step1()
    plane.step1()
    line.step2()
    plane.step2()
    line.step3()
    line.finish()
    load.wait()
    to_plan.wait()

    def ahead(count, begin):
        products(
            count,
            begin,
            lambda t: tiles[within(plan[0, t], SLOTS)],
            lambda t: feats_all[within(plan[1, t], COL_UNITS)],
            lambda t: plan[2, t].astype(F32),
            total,
            sums,
        )

    def back(count, begin, left, rows):
        products(
            count,
            begin,
            lambda t: left[within(plan[4, t], ROW_UNITS)],
            lambda t: tiles[within(plan[3, t], SLOTS)],
            lambda t: plan[5, t].astype(F32),
            total.at[pl.ds(0, rows)],
            sums.at[:, pl.ds(0, rows)],
        )

    def choose(to, rows):
        pick(
            COL_UNITS,
            sums.at[:, pl.ds(0, rows)],
            lambda u: within(plan[8, u], SLOTS),
            lambda u: plan[9, u].astype(F32),
            to,
        )

    ahead(64, 0)
    plane.step3()
    ahead(64, 64)
    plane.step4()
    pick(ROW_UNITS, sums, lambda u: within(plan[6, u], SLOTS), lambda u: plan[7, u].astype(F32), part)
    plane_sum = PlaneSum(net, "ax", part, relay, landed, part2, relay2, landed2)
    plane.step5()
    for k in range(4):
        plane_sum.start(k)
    for k in range(4):
        plane_sum.start_near(k)
    total[...] = jnp.zeros_like(total)
    plane.finish()
    back(SLOTS, 0, cot_all, BS)
    choose(part_x, BS)
    line_sum = LineSum(net, "bt", part_x, swapped, relay_x, landed_x)
    line_sum.start()
    plane_sum.middle(0)
    plane_sum.middle(1)
    line_sum.middle()
    plane_sum.middle(2)
    line_sum.middle_more()
    plane_sum.middle(3)
    plane_sum.close(0)
    line_sum.late()
    plane_sum.close(1)
    plane_sum.close(2)
    plane_sum.close(3)
    plane_sum.late()
    line_sum.arrive()
    plane_sum.arrive()
    half = BS // 2
    early = GatherPlane(net, "p", slope_all_0)
    late = GatherPlane(net, "q", slope_all_1)
    ax_parts, hiddens, grads, back_two = [], [], [], []
    for block in (0, 1):
        back_two.append(line_sum.finish(block).astype(BF))
        d_hidden = DOT(w_two[...], back_two[block])
        ax = jnp.concatenate([plane_sum.finish(block, h) for h in (0, 1)], axis=0).T
        high, low = both(ax)
        pre = DOT(w_one_t[...], high) + DOT(w_one_t[...], low)
        gate = 1.0 / (1.0 + jnp.exp(-pre))
        slope = (d_hidden * gate * (1.0 + pre * (1.0 - gate))).astype(BF)
        grads.append(slope)
        slope_all_0[early.unit(block, 0, 0)] = slope[:half]
        slope_all_1[late.unit(block, 0, 0)] = slope[half:]
        hiddens.append((pre * gate).astype(BF))
        ax_parts.append((high, low))
    early.start()
    total[...] = jnp.zeros_like(total)
    one = jnp.zeros((BS, BS), F32)
    two = jnp.zeros((BS, BS), F32)
    for block in (0, 1):
        two += lax.dot_general(hiddens[block], back_two[block], NT, preferred_element_type=F32)
        for values in ax_parts[block]:
            one += lax.dot_general(values, grads[block], NT, preferred_element_type=F32)
    mine[:BS] = one
    mine[BS:] = two
    early.start_more()
    weights = GradSum(net, mine, swapped_w, from_x, from_y, from_z, done)
    weights.start()
    late.start()
    early.step1()
    early.step2()
    late.start_more()
    early.step3()
    weights.step1()
    early.step4()
    late.step1()
    early.step5()
    late.step2()
    early.finish()
    weights.step2()
    back(64, 0, slope_all_0, half)
    late.step3()
    back(64, 64, slope_all_0, half)
    late.step4()
    line_sum.left()
    part_0, part_1 = (part_x.at[:, pl.ds(h * half, half)] for h in (0, 1))
    choose(part_0, half)
    first = LineSum(net, "s", part_0, swapped_0, relay_0, landed_0)
    second = LineSum(net, "t", part_1, swapped_1, relay_1, landed_1)
    first.start()
    late.step5()
    weights.step3()
    total[...] = jnp.zeros_like(total)
    first.middle()
    first.middle_more()
    late.finish()
    weights.step4()
    back(64, 0, slope_all_1, half)
    first.late()
    back(64, 64, slope_all_1, half)
    choose(part_1, half)
    second.start()
    weights.step5()
    second.middle()
    first.arrive()
    for block in (0, 1):
        back_out[block, :half] = first.finish(block).astype(BF)
    second.middle_more()
    second.late()
    weights.step6()
    for copies in (line, plane, plane_sum, early, late, first):
        copies.left()
    second.arrive()
    for block in (0, 1):
        back_out[block, half:] = second.finish(block).astype(BF)
    weights.finish()
    grads_out[...] = done[...]
    second.left()
    weights.left()


def finish_kernel(back, w_one, grads, input_grad, grad_one, grad_two):
    grad_one[...] = grads[:BS]
    grad_two[...] = grads[BS:]
    for block in (0, 1):
        input_grad[pl.ds(block * BS, BS)] = DOT(w_one[...], back[block]).T.astype(BF)


def write_plan(rows, cols, count, plan):
    shape = (SLOTS, SLOTS)
    down = lax.broadcasted_iota(jnp.int32, shape, 0)
    across = lax.broadcasted_iota(jnp.int32, shape, 1)
    live = down < count

    def tall(ref, top):
        return jnp.broadcast_to(jnp.clip(ref[...], 0, top), shape).T

    def over_slots(where, values):
        return jnp.sum(jnp.where(where, values, 0), axis=0, keepdims=True)

    rows, cols = tall(rows, ROW_UNITS - 1), tall(cols, COL_UNITS - 1)
    for at, last_at, major, minor in ((0, 6, rows, cols), (3, 8, cols, rows)):
        key = jnp.where(live, major * 64 + minor, 4096 + down)
        rank = jnp.sum(jnp.where(key.T < key, 1, 0), axis=1, keepdims=True)
        here = rank == across
        alive = jnp.where(live, major, -1)
        plan[at : at + 1] = over_slots(here, down)
        plan[at + 1 : at + 2] = over_slots(here, minor)
        same = over_slots(here, alive) == over_slots(rank + 1 == across, alive)
        plan[at + 2 : at + 3] = jnp.where(same & (across[:1] > 0), 1, 0)
        plan[last_at : last_at + 1] = jnp.maximum(over_slots(live & (major <= across), 1) - 1, 0)
        plan[last_at + 1 : last_at + 2] = jnp.minimum(over_slots(live & (major == across), 1), 1)


def units(count, rows=BS):
    return pltpu.VMEM((count, rows, BS), BF)


SMEM = pl.BlockSpec(memory_space=pltpu.SMEM)
VMEM = pl.BlockSpec(memory_space=pltpu.VMEM)
ANY = pl.BlockSpec(memory_space=pl.ANY)


def call(rows, cols, count, feats, cot, w_one, w_two, tiles):
    half = BS // 2
    last = [units(ROW_UNITS, half), units(8, half), units(2, half), units(4, half)]
    return pl.pallas_call(
        kernel,
        out_shape=(
            jax.ShapeDtypeStruct((2, BS, BS), BF),
            jax.ShapeDtypeStruct((2 * BS, BS), F32),
        ),
        in_specs=[VMEM, VMEM, SMEM, VMEM, VMEM, VMEM, VMEM, ANY],
        out_specs=(VMEM, VMEM),
        scratch_shapes=[
            pltpu.SMEM((16, SLOTS), jnp.int32),
            pltpu.VMEM((16, SLOTS), jnp.int32),
            units(SLOTS),
            units(SLOTS),
            pltpu.VMEM((BS, BS), F32),
            units(COL_UNITS),
            units(ROW_UNITS),
            units(ROW_UNITS),
            units(16, half),
            units(16),
            units(8),
            units(4, half),
            units(4),
            units(COL_UNITS),
            units(8),
            units(2),
            units(4),
            pltpu.VMEM((BS, BS), BF),
            *last,
            *last,
            pltpu.VMEM((2 * BS, BS), F32),
            pltpu.VMEM((BS, BS), F32),
            pltpu.VMEM((3, 64, BS), F32),
            pltpu.VMEM((3, 16, BS), F32),
            pltpu.VMEM((4, 16, BS), F32),
            pltpu.VMEM((2 * BS, BS), F32),
            pltpu.SemaphoreType.DMA,
            pltpu.SemaphoreType.DMA,
            pltpu.SemaphoreType.DMA((67,)),
        ],
        compiler_params=pltpu.CompilerParams(
            collective_id=0, has_side_effects=True, vmem_limit_bytes=62 * 2**20
        ),
        name="graph_back",
    )(rows, cols, count, feats, cot, w_one, w_two, tiles)


def per_device(
    node_feats, out_grad, weight_one, weight_two, tile_values, tile_rows, tile_cols, tile_count
):
    back, grads = call(
        tile_rows.reshape(1, SLOTS),
        tile_cols.reshape(1, SLOTS),
        tile_count,
        node_feats,
        out_grad,
        weight_one,
        weight_two,
        tile_values,
    )
    return pl.pallas_call(
        finish_kernel,
        out_shape=(
            jax.ShapeDtypeStruct((2 * BS, BS), BF),
            jax.ShapeDtypeStruct((BS, BS), F32),
            jax.ShapeDtypeStruct((BS, BS), F32),
        ),
        in_specs=[VMEM, VMEM, VMEM],
        out_specs=(VMEM, VMEM, VMEM),
        name="finish",
    )(back, weight_one, grads)


def solution(mesh):
    in_specs = (
        P(("row", "col"), None),
        P(("row", "col"), None),
        P(),
        P(),
        P(("row", "col"), None, None),
        P(("row", "col")),
        P(("row", "col")),
        P(("row", "col")),
    )
    out_specs = (P(("row", "col"), None), P(), P())
    return jax.shard_map(
        per_device, mesh=mesh, in_specs=in_specs, out_specs=out_specs, check_vma=False
    )
```

time: 231 us -> 105 us (0.45)
  waiting for transfers between devices: 90.4 us -> 0 us
  between operations: 14.8 us -> 1.29 us
  Pallas kernels: 116 us -> 103 us
  local copies, waits for them, and re-layouts: 4.22 us -> 0 us
  other arithmetic: 3.86 us -> 0 us
    psum x1 -> x0, waiting for transfers between devices: 90.4 us -> none  [per_device(): lax.psum(jnp.concatenate([grad_one, grad_two], axis=0), ('row', 'col'))]
    pallas_call x2, Pallas kernels: 116 us -> 103 us  [the longest x1 101 us: call(): pl.pallas_call(kernel, out_shape=(jax.ShapeDtypeStruct((2, BS, BS), BF),...]
  transfers between devices with their start and end apart: 1 -> 0, of which waited for: 1 -> 0; matrix products, arithmetic and copies ran while one was open for 0% -> 0% of each run, Pallas kernels for 24% -> 0%
where the time goes in v2:
time: 105 us; the launch traced here: 104 us
  Pallas kernels  103 us (98%)
  between operations  1.29 us (1%)
    pallas_call x1, Pallas kernels, call(): pl.pallas_call(kernel, out_shape=(jax.ShapeDtypeStruct((2, BS, BS), BF),...  101 us
    pallas_call x1, Pallas kernels, per_device(): pl.pallas_call(finish_kernel, out_shape=(jax.ShapeDtypeStruct((2 * BS, BS...  2.35 us

profile of v2, /device:TPU:0, one launch (start us, length us, event | category | flops | bytes accessed | tf_op | source)
XLA Modules:
  0.0 104.5 jit_solution(15739002149377195455)
XLA Ops:
  1.3 100.8 %graph_back.1 = (bf16[2,256,256]{2,1,0:T(8,128)(2,1)}, f32[512,256]{1,0:T(8,128)}) custom-call(s32[1,128]{1,0:T(1,128)} %bitcast.2, s32[1,128]{1,0:T(1,128)} %bitcast.3, s32[1]{0:T(128)S(6)} %copy.11.count, bf16[512,256]{1,0:T(8,128)(2,1)} %feats.1, bf16[512,256]{1,0:T(8,128)(2,1)} %cot.1, bf16[256,256]{1,0:T(8,128)(2,1)} %w_one.3, bf16[256,256]{1,0:T(8,128)(2,1)} %w_two.1, ...), custom_call_target="tpu_custom_call" | custom-call | tf_op jit(solution)/shard_map/graph_back/pallas_call | solution.py:709
  102.1 2.3 %finish.1 = (bf16[512,256]{1,0:T(8,128)(2,1)}, f32[256,256]{1,0:T(8,128)}, f32[256,256]{1,0:T(8,128)}) custom-call(bf16[2,256,256]{2,1,0:T(8,128)(2,1)} %get-tuple-element.5.back, bf16[256,256]{1,0:T(8,128)(2,1)} %w_one.3, f32[512,256]{1,0:T(8,128)} %get-tuple-element.6.grads), custom_call_target="tpu_custom_call" | custom-call | tf_op jit(solution)/shard_map/finish/pallas_call | solution.py:768

commit v3 on v2

--- a/solution.py
+++ b/solution.py
@@ -14,6 +14,7 @@
 ROW_UNITS = 32
 COL_UNITS = 16
 UNROLL = 16
+EARLY = 128
 WAYS = (1, -1)
 DOT = functools.partial(jnp.dot, preferred_element_type=F32)
 ROWS_OF_HALF = {1: 0, -1: 1}
@@ -92,10 +93,11 @@
         return self.buf.at[self.unit(block, first, second), rows]
 
     def put(self, key, ref, axis, way):
-        self.net.send(self.tag, (self.tag, *key), ref, ref, axis, way)
+        leave = (self.tag, "a" if key == ("a",) else "rest")
+        self.net.send(leave, (self.tag, *key), ref, ref, axis, way)
 
     def get(self, key, count):
-        self.net.got(self.tag, (self.tag, *key), self.buf.at[pl.ds(0, count)])
+        self.net.got((self.tag, "a"), (self.tag, *key), self.buf.at[pl.ds(0, count)])
 
     def spread(self, block, first):
         two = self.axes(block)[1]
@@ -147,8 +149,11 @@
     def finish(self):
         self.get(("e",), 8)
 
+    def left_first(self):
+        self.net.left((self.tag, "a"), (self.tag, "a"), self.buf.at[pl.ds(0, 4)])
+
     def left(self):
-        self.net.left(self.tag, (self.tag, "a"), self.buf.at[pl.ds(0, 30)])
+        self.net.left((self.tag, "rest"), (self.tag, "a"), self.buf.at[pl.ds(0, 26)])
 
 
 class GatherLine:
@@ -205,7 +210,7 @@
         self.half, self.relay, self.landed, self.more = half, relay, landed, more
 
     def send(self, at, src, dst, way):
-        self.net.send(self.tag, self.keys[at], src, dst, self.axis, way)
+        self.net.send((self.tag, at), self.keys[at], src, dst, self.axis, way)
 
     def term(self, step, h):
         value = self.half(step, h)[...].astype(F32)
@@ -253,13 +258,13 @@
         return (self.net.off("x", step) * 2 + core) * 2
 
     def get(self, kind, ref):
-        self.net.got(self.tag, (self.tag, kind), ref)
+        self.net.got((self.tag, 0), (self.tag, kind), ref)
 
     def start(self):
         for step in (2, 1, -1, 0):
             src = self.part.at[pl.ds(self.first(step, 1 - self.net.core), 2)]
             dst = self.swapped.at[pl.ds(self.net.off("x", step) * 2, 2)]
-            self.net.send(self.tag, (self.tag, "s" if step == 2 else "u"), src, dst, "core", 0)
+            self.net.send((self.tag, 1), (self.tag, "s" if step == 2 else "u"), src, dst, "core", 0)
 
     def join(self, step, h):
         self.part[self.first(step, self.net.core) + h] = self.ring.term(step, h).astype(BF)
@@ -274,6 +279,9 @@
         self.get("u", self.swapped.at[pl.ds(0, 6)])
         for way in WAYS:
             self.join(way, 1 - ROWS_OF_HALF[way])
+
+    def near(self):
+        self.net.left((self.tag, 0), (self.tag, "s"), self.relay)
         self.ring.start_near()
 
     def late(self):
@@ -287,7 +295,7 @@
         return self.ring.finish(h)
 
     def left(self):
-        self.net.left(self.tag, (self.tag, "s"), self.part.at[pl.ds(0, 14)])
+        self.net.left((self.tag, 1), (self.tag, "s"), self.part.at[pl.ds(0, 12)])
 
 
 class PlaneSum:
@@ -335,7 +343,7 @@
             )
 
     def get(self, kind, k, count):
-        self.net.got(self.tag, (self.tag, kind, k), self.part.at[pl.ds(0, count)])
+        self.net.got((self.tag, 0), (self.tag, kind, k), self.part.at[pl.ds(0, count)])
 
     def start(self, k):
         for block in (0, 1):
@@ -374,7 +382,8 @@
         return self.last[block].finish(h)
 
     def left(self):
-        self.net.left(self.tag, (self.tag, "p", 0), self.part.at[pl.ds(0, 30)])
+        self.net.left((self.tag, 0), (self.tag, "p", 0), self.part.at[pl.ds(0, 10)])
+        self.net.left((self.tag, 1), (self.tag, "p", 0), self.part.at[pl.ds(0, 20)])
 
 
 class GradSum:
@@ -423,44 +432,45 @@
 
     def step4(self):
         self.get(3, self.from_z.at[pl.ds(0, 3)])
-        ref = self.done.at[self.rows(0, 0, 0)]
+        at = self.net.at
+        ref = self.done.at[self.net.core, at["x"], at["y"]]
         ref[...] = (self.from_z[0] + self.from_z[1]) + (self.from_z[2] + self.from_z[3])
         for step in self.FAR:
-            self.put(4, ref, ref, "y", step)
+            self.put(4, ref, ref, "x", step)
 
     def step5(self):
-        self.get(4, self.done.at[pl.ds(0, 48)])
-        ref = self.done.at[self.rows(0, 0)]
+        self.get(4, self.from_y)
+        ref = self.done.at[self.net.core, :, self.net.at["y"]]
         for step in self.FAR:
-            self.put(5, ref, ref, "x", step)
+            self.put(5, ref, ref, "y", step)
 
     def step6(self):
-        self.get(5, self.done.at[pl.ds(0, 192)])
-        ref = self.done.at[self.rows(0)]
+        self.get(5, self.from_x)
+        ref = self.done.at[self.net.core]
         self.put(6, ref, ref, "core", 0)
 
     def finish(self):
         self.get(6, self.swapped)
 
     def left(self):
-        for axis, rows in (("core", 512), ("x", 384), ("y", 96), ("z", 48)):
-            self.net.left(("w", axis), ("w", 0), self.done.at[pl.ds(0, rows)])
+        for axis, rows in (("core", 512), ("x", 240), ("y", 240), ("z", 48)):
+            self.net.left(("w", axis), ("w", 0), self.mine.at[pl.ds(0, rows)])
 
 
 def within(index, count):
     return jnp.clip(index, 0, count - 1)
 
 
-def products(count, begin, left, right, keep, total, sums):
+def products(count, begin, left, right, keep, total, sums, unroll=UNROLL):
     def body(step, carry):
-        for turn in range(UNROLL):
-            t = begin + step * UNROLL + turn
+        for turn in range(unroll):
+            t = begin + step * unroll + turn
             value = total[...] * keep(t) + DOT(left(t), right(t))
             total[...] = value
             sums[t] = value.astype(BF)
         return carry
 
-    lax.fori_loop(0, count // UNROLL, body, 0)
+    lax.fori_loop(0, count // unroll, body, 0)
 
 
 def pick(units, sums, last, some, part):
@@ -480,31 +490,41 @@
 
 
 def kernel(
-    rows, cols, count, feats, cot, w_one, w_two, tiles_hbm, back_out, grads_out,
-    plan, plan_wide, tiles, sums, total, feats_all, cot_all, part, relay, landed, part2, relay2, landed2,
+    rows_in, cols_in, count, feats, cot_in, w_one_in, w_two_in, tiles_hbm, back_out, grads_out,
+    rows, cols, cot, w_one, w_two, plan, plan_wide, tiles, sums, total, feats_all, cot_all, part, relay, landed, part2, relay2, landed2,
     part_x, swapped, relay_x, landed_x, w_one_t,
     slope_all_0, swapped_0, relay_0, landed_0,
     slope_all_1, swapped_1, relay_1, landed_1,
-    mine, swapped_w, from_x, from_y, from_z, done, tile_sem, plan_sem, sems,
+    mine, swapped_w, from_x, from_y, from_z, done, tile_sem, plan_sem, cot_sem, feats_sem, small_sem, grads_sem, sems,
 ):
     net = Net(sems)
     net.greet()
-    load = pltpu.make_async_copy(tiles_hbm, tiles, tile_sem)
-    load.start()
     line = GatherLine(net, "x", feats_all)
     plane = GatherPlane(net, "g", cot_all)
+    loads = [pltpu.make_async_copy(cot_in, cot, cot_sem)]
     for block in (0, 1):
         span = pl.ds(block * BS, BS)
-        feats_all[line.first(0, net.core) + block] = feats[span]
+        own = feats_all.at[line.first(0, net.core) + block]
+        loads.append(pltpu.make_async_copy(feats.at[span], own, feats_sem.at[block]))
+    for at, (src, dst) in enumerate(((rows_in, rows), (cols_in, cols), (w_one_in, w_one), (w_two_in, w_two))):
+        loads.append(pltpu.make_async_copy(src, dst, small_sem.at[at]))
+    loads.append(pltpu.make_async_copy(tiles_hbm, tiles, tile_sem))
+    for load in loads:
+        load.start()
+    loads[0].wait()
+    for block in (0, 1):
+        span = pl.ds(block * BS, BS)
         cot_all[plane.unit(block, 0, 0)] = cot[span].astype(F32).T.astype(BF)
+    for load in loads[1:-1]:
+        load.wait()
+    w_one_t[...] = w_one[...].astype(F32).T.astype(BF)
+    total[...] = jnp.zeros_like(total)
+    write_plan(rows, cols, count[0], plan_wide)
+    to_plan = pltpu.make_async_copy(plan_wide, plan, plan_sem)
+    to_plan.start()
     net.met()
     line.start()
     plane.start()
-    write_plan(rows, cols, count[0], plan_wide)
-    to_plan = pltpu.make_async_copy(plan_wide, plan, plan_sem)
-    to_plan.start()
-    w_one_t[...] = w_one[...].astype(F32).T.astype(BF)
-    total[...] = jnp.zeros_like(total)
     line.start_more()
     plane.start_more()
     line.step1()
@@ -513,7 +533,7 @@
     plane.step2()
     line.step3()
     line.finish()
-    load.wait()
+    loads[-1].wait()
     to_plan.wait()
 
     def ahead(count, begin):
@@ -527,7 +547,7 @@
             sums,
         )
 
-    def back(count, begin, left, rows):
+    def back(count, begin, left, rows, unroll=UNROLL):
         products(
             count,
             begin,
@@ -536,6 +556,7 @@
             lambda t: plan[5, t].astype(F32),
             total.at[pl.ds(0, rows)],
             sums.at[:, pl.ds(0, rows)],
+            unroll,
         )
 
     def choose(to, rows):
@@ -570,6 +591,7 @@
     plane_sum.middle(2)
     line_sum.middle_more()
     plane_sum.middle(3)
+    line_sum.near()
     plane_sum.close(0)
     line_sum.late()
     plane_sum.close(1)
@@ -578,7 +600,6 @@
     plane_sum.late()
     line_sum.arrive()
     plane_sum.arrive()
-    half = BS // 2
     early = GatherPlane(net, "p", slope_all_0)
     late = GatherPlane(net, "q", slope_all_1)
     ax_parts, hiddens, grads, back_two = [], [], [], []
@@ -591,8 +612,8 @@
         gate = 1.0 / (1.0 + jnp.exp(-pre))
         slope = (d_hidden * gate * (1.0 + pre * (1.0 - gate))).astype(BF)
         grads.append(slope)
-        slope_all_0[early.unit(block, 0, 0)] = slope[:half]
-        slope_all_1[late.unit(block, 0, 0)] = slope[half:]
+        slope_all_0[early.unit(block, 0, 0)] = slope[:EARLY]
+        slope_all_1[late.unit(block, 0, 0)] = slope[EARLY:]
         hiddens.append((pre * gate).astype(BF))
         ax_parts.append((high, low))
     early.start()
@@ -605,60 +626,66 @@
             one += lax.dot_general(values, grads[block], NT, preferred_element_type=F32)
     mine[:BS] = one
     mine[BS:] = two
-    early.start_more()
     weights = GradSum(net, mine, swapped_w, from_x, from_y, from_z, done)
     weights.start()
+    early.left_first()
+    early.start_more()
     late.start()
+    weights.step1()
     early.step1()
     early.step2()
+    weights.step2()
     late.start_more()
     early.step3()
-    weights.step1()
     early.step4()
     late.step1()
     early.step5()
+    weights.step3()
     late.step2()
+    late.step3()
+    late.step4()
     early.finish()
-    weights.step2()
-    back(64, 0, slope_all_0, half)
-    late.step3()
-    back(64, 64, slope_all_0, half)
-    late.step4()
+    back(32, 0, slope_all_0, EARLY, 32)
+    late.step5()
+    weights.step4()
+    back(96, 32, slope_all_0, EARLY, 32)
+    weights.step5()
     line_sum.left()
-    part_0, part_1 = (part_x.at[:, pl.ds(h * half, half)] for h in (0, 1))
-    choose(part_0, half)
+    part_0, part_1 = part_x.at[:, pl.ds(0, EARLY)], part_x.at[:, pl.ds(EARLY, BS - EARLY)]
+    choose(part_0, EARLY)
     first = LineSum(net, "s", part_0, swapped_0, relay_0, landed_0)
     second = LineSum(net, "t", part_1, swapped_1, relay_1, landed_1)
     first.start()
-    late.step5()
-    weights.step3()
     total[...] = jnp.zeros_like(total)
+    late.finish()
+    back(32, 0, slope_all_1, BS - EARLY, 32)
     first.middle()
     first.middle_more()
-    late.finish()
-    weights.step4()
-    back(64, 0, slope_all_1, half)
+    back(96, 32, slope_all_1, BS - EARLY, 32)
+    first.near()
+    choose(part_1, BS - EARLY)
+    second.start()
     first.late()
-    back(64, 64, slope_all_1, half)
-    choose(part_1, half)
-    second.start()
-    weights.step5()
+    weights.step6()
     second.middle()
+    second.middle_more()
+    second.near()
+    weights.finish()
+    keep = pltpu.make_async_copy(done, grads_out, grads_sem)
+    keep.start()
     first.arrive()
     for block in (0, 1):
-        back_out[block, :half] = first.finish(block).astype(BF)
-    second.middle_more()
+        back_out[block, :EARLY] = first.finish(block).astype(BF)
     second.late()
-    weights.step6()
-    for copies in (line, plane, plane_sum, early, late, first):
+    late.left_first()
+    plane.left_first()
+    for copies in (line, plane, plane_sum, early, late, first, weights):
         copies.left()
+    keep.wait()
     second.arrive()
     for block in (0, 1):
-        back_out[block, half:] = second.finish(block).astype(BF)
-    weights.finish()
-    grads_out[...] = done[...]
+        back_out[block, EARLY:] = second.finish(block).astype(BF)
     second.left()
-    weights.left()
 
 
 def finish_kernel(back, w_one, grads, input_grad, grad_one, grad_two):
@@ -705,16 +732,24 @@
 
 def call(rows, cols, count, feats, cot, w_one, w_two, tiles):
     half = BS // 2
-    last = [units(ROW_UNITS, half), units(8, half), units(2, half), units(4, half)]
+
+    def last(rows):
+        return [units(ROW_UNITS, rows), units(8, rows), units(2, rows), units(4, rows)]
+
     return pl.pallas_call(
         kernel,
         out_shape=(
             jax.ShapeDtypeStruct((2, BS, BS), BF),
-            jax.ShapeDtypeStruct((2 * BS, BS), F32),
+            jax.ShapeDtypeStruct((2, 4, 4, 16, BS), F32),
         ),
-        in_specs=[VMEM, VMEM, SMEM, VMEM, VMEM, VMEM, VMEM, ANY],
-        out_specs=(VMEM, VMEM),
+        in_specs=[ANY, ANY, SMEM, ANY, ANY, ANY, ANY, ANY],
+        out_specs=(VMEM, ANY),
         scratch_shapes=[
+            pltpu.VMEM((1, SLOTS), jnp.int32),
+            pltpu.VMEM((1, SLOTS), jnp.int32),
+            pltpu.VMEM((2 * BS, BS), BF),
+            pltpu.VMEM((BS, BS), BF),
+            pltpu.VMEM((BS, BS), BF),
             pltpu.SMEM((16, SLOTS), jnp.int32),
             pltpu.VMEM((16, SLOTS), jnp.int32),
             units(SLOTS),
@@ -733,17 +768,21 @@
             units(2),
             units(4),
             pltpu.VMEM((BS, BS), BF),
-            *last,
-            *last,
+            *last(EARLY),
+            *last(BS - EARLY),
             pltpu.VMEM((2 * BS, BS), F32),
             pltpu.VMEM((BS, BS), F32),
             pltpu.VMEM((3, 64, BS), F32),
             pltpu.VMEM((3, 16, BS), F32),
             pltpu.VMEM((4, 16, BS), F32),
-            pltpu.VMEM((2 * BS, BS), F32),
+            pltpu.VMEM((2, 4, 4, 16, BS), F32),
             pltpu.SemaphoreType.DMA,
             pltpu.SemaphoreType.DMA,
-            pltpu.SemaphoreType.DMA((67,)),
+            pltpu.SemaphoreType.DMA,
+            pltpu.SemaphoreType.DMA((2,)),
+            pltpu.SemaphoreType.DMA((4,)),
+            pltpu.SemaphoreType.DMA,
+            pltpu.SemaphoreType.DMA((76,)),
         ],
         compiler_params=pltpu.CompilerParams(
             collective_id=0, has_side_effects=True, vmem_limit_bytes=62 * 2**20
@@ -775,7 +814,7 @@
         in_specs=[VMEM, VMEM, VMEM],
         out_specs=(VMEM, VMEM, VMEM),
         name="finish",
-    )(back, weight_one, grads)
+    )(back, weight_one, grads.reshape(2 * BS, BS))
 
 
 def solution(mesh):

time: 105 us -> 101 us (0.962)
  Pallas kernels: 103 us -> 99.3 us
    pallas_call x1, Pallas kernels: 101 us -> 97 us  [call(): pl.pallas_call(kernel, out_shape=(jax.ShapeDtypeStruct((2, BS, BS), BF),...]
where the time goes in v3:
time: 101 us
  Pallas kernels  99.3 us (98%)
  between operations  1.29 us (1%)
    pallas_call x1, Pallas kernels, call(): pl.pallas_call(kernel, out_shape=(jax.ShapeDtypeStruct((2, BS, BS), BF),...  97 us
    pallas_call x1, Pallas kernels, per_device(): pl.pallas_call(finish_kernel, out_shape=(jax.ShapeDtypeStruct((2 * BS, BS...  2.35 us

profile of v3, /device:TPU:0, one launch (start us, length us, event | category | flops | bytes accessed | tf_op | source)
XLA Modules:
  0.0 100.6 jit_solution(7870492399642097115)
XLA Ops:
  1.3 97.0 %graph_back.1 = (bf16[2,256,256]{2,1,0:T(8,128)(2,1)}, f32[2,4,4,16,256]{4,3,2,1,0:T(8,128)}) custom-call(s32[1,128]{1,0:T(1,128)} %bitcast.4, s32[1,128]{1,0:T(1,128)} %bitcast.5, s32[1]{0:T(128)S(6)} %copy.11.count, bf16[512,256]{1,0:T(8,128)(2,1)} %feats.1, bf16[512,256]{1,0:T(8,128)(2,1)} %cot_in.1, bf16[256,256]{1,0:T(8,128)(2,1)} %w_one.1, ...), custom_call_target="tpu_custom_call" | custom-call | tf_op jit(solution)/shard_map/graph_back/pallas_call | solution.py:739
  98.2 2.3 %finish.1 = (bf16[512,256]{1,0:T(8,128)(2,1)}, f32[256,256]{1,0:T(8,128)}, f32[256,256]{1,0:T(8,128)}) custom-call(bf16[2,256,256]{2,1,0:T(8,128)(2,1)} %get-tuple-element.5.back, bf16[256,256]{1,0:T(8,128)(2,1)} %w_one.1, f32[512,256]{1,0:T(8,128)} %bitcast.3), custom_call_target="tpu_custom_call" | custom-call | tf_op jit(solution)/shard_map/finish/pallas_call | solution.py:807

commit v4 on v3

--- a/solution.py
+++ b/solution.py
@@ -13,7 +13,7 @@
 SLOTS = 128
 ROW_UNITS = 32
 COL_UNITS = 16
-UNROLL = 16
+UNROLL = 32
 EARLY = 128
 WAYS = (1, -1)
 DOT = functools.partial(jnp.dot, preferred_element_type=F32)
@@ -574,30 +574,35 @@
     plane.step4()
     pick(ROW_UNITS, sums, lambda u: within(plan[6, u], SLOTS), lambda u: plan[7, u].astype(F32), part)
     plane_sum = PlaneSum(net, "ax", part, relay, landed, part2, relay2, landed2)
+    plane_sum.start(0)
     plane.step5()
-    for k in range(4):
-        plane_sum.start(k)
-    for k in range(4):
-        plane_sum.start_near(k)
+    plane_sum.start_near(0)
+    plane_sum.start(1)
+    plane_sum.start(2)
     total[...] = jnp.zeros_like(total)
     plane.finish()
-    back(SLOTS, 0, cot_all, BS)
+    plane_sum.start_near(1)
+    plane_sum.start_near(2)
+    back(64, 0, cot_all, BS)
+    plane_sum.middle(0)
+    plane_sum.start(3)
+    plane_sum.start_near(3)
+    back(64, 64, cot_all, BS)
     choose(part_x, BS)
     line_sum = LineSum(net, "bt", part_x, swapped, relay_x, landed_x)
     line_sum.start()
-    plane_sum.middle(0)
     plane_sum.middle(1)
+    plane_sum.middle(2)
     line_sum.middle()
-    plane_sum.middle(2)
     line_sum.middle_more()
+    plane_sum.close(0)
     plane_sum.middle(3)
     line_sum.near()
-    plane_sum.close(0)
+    plane_sum.close(1)
     line_sum.late()
-    plane_sum.close(1)
     plane_sum.close(2)
+    plane_sum.late()
     plane_sum.close(3)
-    plane_sum.late()
     line_sum.arrive()
     plane_sum.arrive()
     early = GatherPlane(net, "p", slope_all_0)
@@ -649,7 +654,6 @@
     late.step5()
     weights.step4()
     back(96, 32, slope_all_0, EARLY, 32)
-    weights.step5()
     line_sum.left()
     part_0, part_1 = part_x.at[:, pl.ds(0, EARLY)], part_x.at[:, pl.ds(EARLY, BS - EARLY)]
     choose(part_0, EARLY)
@@ -659,24 +663,26 @@
     total[...] = jnp.zeros_like(total)
     late.finish()
     back(32, 0, slope_all_1, BS - EARLY, 32)
+    weights.step5()
     first.middle()
     first.middle_more()
-    back(96, 32, slope_all_1, BS - EARLY, 32)
+    back(64, 32, slope_all_1, BS - EARLY, 32)
     first.near()
+    back(32, 96, slope_all_1, BS - EARLY, 32)
     choose(part_1, BS - EARLY)
     second.start()
     first.late()
-    weights.step6()
     second.middle()
     second.middle_more()
     second.near()
-    weights.finish()
-    keep = pltpu.make_async_copy(done, grads_out, grads_sem)
-    keep.start()
+    weights.step6()
     first.arrive()
     for block in (0, 1):
         back_out[block, :EARLY] = first.finish(block).astype(BF)
     second.late()
+    weights.finish()
+    keep = pltpu.make_async_copy(done, grads_out, grads_sem)
+    keep.start()
     late.left_first()
     plane.left_first()
     for copies in (line, plane, plane_sum, early, late, first, weights):

time: 101 us -> 98.2 us (0.972)
  Pallas kernels: 99.3 us -> 96.7 us
    pallas_call x1, Pallas kernels: 97 us -> 94.4 us  [call(): pl.pallas_call(kernel, out_shape=(jax.ShapeDtypeStruct((2, BS, BS), BF),...]
where the time goes in v4:
time: 98.2 us; the launch traced here: 98 us
  Pallas kernels  96.7 us (98%)
  between operations  1.29 us (1%)
    pallas_call x1, Pallas kernels, call(): pl.pallas_call(kernel, out_shape=(jax.ShapeDtypeStruct((2, BS, BS), BF),...  94.4 us
    pallas_call x1, Pallas kernels, per_device(): pl.pallas_call(finish_kernel, out_shape=(jax.ShapeDtypeStruct((2 * BS, BS...  2.35 us

profile of v4, /device:TPU:0, one launch (start us, length us, event | category | flops | bytes accessed | tf_op | source)
XLA Modules:
  0.0 98.0 jit_solution(15650858636774436864)
XLA Ops:
  1.3 94.4 %graph_back.1 = (bf16[2,256,256]{2,1,0:T(8,128)(2,1)}, f32[2,4,4,16,256]{4,3,2,1,0:T(8,128)}) custom-call(s32[1,128]{1,0:T(1,128)} %bitcast.4, s32[1,128]{1,0:T(1,128)} %bitcast.5, s32[1]{0:T(128)S(6)} %copy.11.count, bf16[512,256]{1,0:T(8,128)(2,1)} %feats.1, bf16[512,256]{1,0:T(8,128)(2,1)} %cot_in.1, bf16[256,256]{1,0:T(8,128)(2,1)} %w_one.1, ...), custom_call_target="tpu_custom_call" | custom-call | tf_op jit(solution)/shard_map/graph_back/pallas_call | solution.py:745
  95.7 2.3 %finish.1 = (bf16[512,256]{1,0:T(8,128)(2,1)}, f32[256,256]{1,0:T(8,128)}, f32[256,256]{1,0:T(8,128)}) custom-call(bf16[2,256,256]{2,1,0:T(8,128)(2,1)} %get-tuple-element.5.back, bf16[256,256]{1,0:T(8,128)(2,1)} %w_one.1, f32[512,256]{1,0:T(8,128)} %bitcast.3), custom_call_target="tpu_custom_call" | custom-call | tf_op jit(solution)/shard_map/finish/pallas_call | solution.py:813
